TPU v7x, 512 devices: a whole 4x8x8 slice. The times are simulated.
512 devices in a mesh: replica: 64 (over z, y), tensor: 8 (over x, core).
Axes of the slice: x: 4, y: 8, z: 8, core: 2. Of those that a mesh axis runs over, the one named last changes fastest.
Arguments:
- mamba_in: bfloat16 [1024, 3, 2, 8192], P('replica', None, None, 'tensor'), may hold values from -6 to 6
- queries: bfloat16 [1024, 3, 8, 1024], P('replica', None, 'tensor'), may hold values from -400 to 400
- new_kv: bfloat16 [1024, 3, 8, 256], P('replica', None, 'tensor'), may hold values from -6 to 6
- ssm_state: float32 [1024, 16, 8192], P('replica', None, 'tensor'), may hold values from -4 to 4
- kv_cache: bfloat16 [1024, 16, 8, 256], P('replica', None, 'tensor'), may hold values from -16 to 16
- lengths: int32 [1024], P('replica'), may hold values from 1 to 16, 8192 in all
- destination: int32 [1024, 1], P('replica'), may hold values from 0 to 63; in each aligned block of 16 rows (0 to 15, 16 to 31, ...) no two rows name the same one
- xproj_w: bfloat16 [8192, 544], P('tensor'), may hold values from -0.0625 to 0.0625
- dtproj_w: bfloat16 [512, 8192], P(None, 'tensor'), may hold values from -0.25 to 0.25
- dt_bias: float32 [8192], P('tensor'), may hold values from -5 to -2
- a_log: float32 [16, 8192], P(None, 'tensor'), may hold values from 0 to 2.77
- d_skip: float32 [8192], P('tensor'), may hold values from 0.1 to 1.9
Outputs:
- mixed: bfloat16 [4096, 3, 8192], P('replica', None, 'tensor')
- attended: bfloat16 [4096, 3, 8, 1024], P('replica', None, 'tensor')
- moved_state: bfloat16 [4096, 16, 8192], P('replica', None, 'tensor')
- moved_pages: bfloat16 [4096, 19, 8, 256], P('replica', None, 'tensor')
Inputs may be any that keep to these rules, and one draw needn't show every extreme that they name: `destination`: among the 16 rows of one replica, no replica is named more than 1 times; every replica takes some row.
All inputs are finite; a program needn't handle non-finite values. No bound on the sum of `lengths` on one device may be relied on, other than what follows from the above.
Results may differ from a plain program's by a relative error of at most 0.0075.
Values may be sent and summed in bfloat16 or wider, within the bound.
A program may use at most 64 MiB of HBM per device.

v0:
```python
import jax
import jax.numpy as jnp
from jax import lax
from jax.sharding import PartitionSpec as P


def place_rows(source_rows, chosen, present):
    gathered = jnp.take(source_rows, chosen, axis=0)
    keeper = present.reshape((present.shape[0],) + (1,) * (source_rows.ndim - 1))
    return jnp.where(keeper, gathered, jnp.zeros_like(gathered))


def extend_pages(kv_pages, new_kv, lengths):
    row_count = kv_pages.shape[0]
    step_count = new_kv.shape[1]
    padding = jnp.zeros((row_count, step_count) + kv_pages.shape[2:], kv_pages.dtype)
    grown = jnp.concatenate([kv_pages, padding], axis=1)
    position = jnp.arange(grown.shape[1], dtype=jnp.int32)[None, :]
    for offset in range(step_count):
        hit = (position == lengths[:, None] + offset)[:, :, None, None]
        grown = jnp.where(hit, new_kv[:, offset][:, None], grown)
    return grown


def decode(
    mamba_rows,
    queries,
    new_kv,
    ssm_carry,
    kv_pages,
    lengths,
    xproj_w,
    dtproj_w,
    dt_bias,
    a_log,
    d_skip,
):
    slot_count = mamba_rows.shape[0]
    step_count = mamba_rows.shape[1]
    low_width = dtproj_w.shape[0]
    state_size = a_log.shape[0]
    head_count = kv_pages.shape[2]
    head_width = kv_pages.shape[3] // 2
    group_size = queries.shape[3] // head_width
    context = kv_pages.shape[1]
    decay_rate = -jnp.exp(a_log)
    score_scale = head_width ** (-0.5)
    cache_keys = kv_pages[..., :head_width]
    cache_vals = kv_pages[..., head_width:]
    fresh_keys = new_kv[..., :head_width]
    fresh_vals = new_kv[..., head_width:]
    cache_mask = (jnp.arange(context, dtype=jnp.int32)[None, :] < lengths[:, None])[
        :, None, None, :
    ]
    mixed_steps = []
    attended_steps = []
    for step_index in range(step_count):
        x_in = mamba_rows[:, step_index, 0]
        z_in = mamba_rows[:, step_index, 1]
        projected = lax.psum(jnp.dot(x_in, xproj_w, preferred_element_type=jnp.float32), "tensor")
        low_rank = projected[:, :low_width].astype(jnp.bfloat16)
        b_vector = projected[:, low_width : low_width + state_size]
        c_vector = projected[:, low_width + state_size :]
        step_size = jax.nn.softplus(
            jnp.dot(low_rank, dtproj_w, preferred_element_type=jnp.float32) + dt_bias
        )
        x_float = x_in.astype(jnp.float32)
        ssm_carry = (
            jnp.exp(step_size[:, None, :] * decay_rate[None]) * ssm_carry
            + b_vector[:, :, None] * (step_size * x_float)[:, None, :]
        )
        readout = (
            jnp.einsum("nsc,ns->nc", ssm_carry, c_vector, precision=lax.Precision.HIGHEST)
            + d_skip * x_float
        )
        mixed_steps.append((readout * jax.nn.silu(z_in.astype(jnp.float32))).astype(jnp.bfloat16))
        query = queries[:, step_index].reshape(slot_count, head_count, group_size, head_width)
        cache_scores = (
            jnp.einsum("nhgd,nkhd->nhgk", query, cache_keys, preferred_element_type=jnp.float32)
            * score_scale
        )
        fresh_scores = (
            jnp.einsum("nhgd,nkhd->nhgk", query, fresh_keys, preferred_element_type=jnp.float32)
            * score_scale
        )
        fresh_mask = (jnp.arange(step_count) <= step_index)[None, None, None, :]
        row_max = jnp.maximum(
            jnp.max(jnp.where(cache_mask, cache_scores, -1e30), axis=-1),
            jnp.max(jnp.where(fresh_mask, fresh_scores, -1e30), axis=-1),
        )
        cache_exp = jnp.where(cache_mask, jnp.exp(cache_scores - row_max[..., None]), 0.0)
        fresh_exp = jnp.where(fresh_mask, jnp.exp(fresh_scores - row_max[..., None]), 0.0)
        denominator = jnp.sum(cache_exp, axis=-1) + jnp.sum(fresh_exp, axis=-1)
        cache_weights = (cache_exp / denominator[..., None]).astype(jnp.bfloat16)
        fresh_weights = (fresh_exp / denominator[..., None]).astype(jnp.bfloat16)
        summed = jnp.einsum(
            "nhgk,nkhd->nhgd", cache_weights, cache_vals, preferred_element_type=jnp.float32
        )
        summed = summed + jnp.einsum(
            "nhgk,nkhd->nhgd", fresh_weights, fresh_vals, preferred_element_type=jnp.float32
        )
        attended_steps.append(
            summed.reshape(slot_count, head_count, group_size * head_width).astype(jnp.bfloat16)
        )
    grown = extend_pages(kv_pages, new_kv, lengths)
    return (
        jnp.stack(mixed_steps, axis=1),
        jnp.stack(attended_steps, axis=1),
        ssm_carry.astype(jnp.bfloat16),
        grown,
    )


def per_device(
    mamba_in,
    queries,
    new_kv,
    ssm_state,
    kv_cache,
    lengths,
    destination,
    xproj_w,
    dtproj_w,
    dt_bias,
    a_log,
    d_skip,
):
    peer_count = lax.axis_size("replica")
    row_count = destination.shape[0]
    capacity = (row_count + peer_count - 1) // peer_count
    targets = destination[:, 0]
    row_ids = jnp.arange(row_count, dtype=jnp.int32)
    earlier = row_ids[None, :] < row_ids[:, None]
    same = targets[:, None] == targets[None, :]
    rank = jnp.sum((same & earlier).astype(jnp.int32), axis=1)
    send_slot = targets * capacity + rank
    slot_ids = jnp.arange(peer_count * capacity, dtype=jnp.int32)
    matches = send_slot[None, :] == slot_ids[:, None]
    present = jnp.any(matches, axis=1)
    chosen = jnp.sum(jnp.where(matches, row_ids[None, :], 0), axis=1)
    carried, arrived_lengths = (
        lax.all_to_all(
            place_rows(ssm_state, chosen, present),
            "replica",
            split_axis=0,
            concat_axis=0,
            tiled=True,
        ),
        lax.all_to_all(
            place_rows(lengths, chosen, present), "replica", split_axis=0, concat_axis=0, tiled=True
        ),
    )
    rows_in, queries_in, fresh_in, pages_in = (
        lax.all_to_all(
            place_rows(mamba_in, chosen, present),
            "replica",
            split_axis=0,
            concat_axis=0,
            tiled=True,
        ),
        lax.all_to_all(
            place_rows(queries, chosen, present), "replica", split_axis=0, concat_axis=0, tiled=True
        ),
        lax.all_to_all(
            place_rows(new_kv, chosen, present), "replica", split_axis=0, concat_axis=0, tiled=True
        ),
        lax.all_to_all(
            place_rows(kv_cache, chosen, present),
            "replica",
            split_axis=0,
            concat_axis=0,
            tiled=True,
        ),
    )
    mixed, attended, moved_state, moved_pages = decode(
        rows_in,
        queries_in,
        fresh_in,
        carried,
        pages_in,
        arrived_lengths,
        xproj_w,
        dtproj_w,
        dt_bias,
        a_log,
        d_skip,
    )
    return (mixed, attended, moved_state, moved_pages)


def solution(mesh):
    placed = (
        P("replica", None, None, "tensor"),
        P("replica", None, "tensor", None),
        P("replica", None, "tensor", None),
        P("replica", None, "tensor"),
        P("replica", None, "tensor", None),
        P("replica"),
        P("replica", None),
        P("tensor", None),
        P(None, "tensor"),
        P("tensor"),
        P(None, "tensor"),
        P("tensor"),
    )
    return jax.shard_map(
        per_device,
        mesh=mesh,
        in_specs=placed,
        out_specs=(
            P("replica", None, "tensor"),
            P("replica", None, "tensor", None),
            P("replica", None, "tensor"),
            P("replica", None, "tensor", None),
        ),
        check_vma=False,
    )
```

profile of v0, /device:TPU:112, one launch (start us, length us, event | category | flops | bytes accessed | tf_op | source)
XLA Modules:
  0.0 288.3 jit_solution(12307950197281650110)
XLA Ops:
  7.2 1.0 convert_reduce_fusion
  8.2 0.7 bitcast_add_fusion
  9.0 1.4 gather_fusion.2
  10.5 0.7 copy.69
  11.2 15.1 %all-to-all-start.2 = ((s32[64,1,1]{2,1,0:T(1,128)}), s32[64,1,1]{2,1,0:T(1,128)S(1)}, u32[]{:S(2)}, u32[]{:S(2)}) async-start(s32[64,1,1]{2,1,0:T(1,128)} %copy.69), calls=%async_computation.2 | async-start | bytes 65536 | tf_op jit(solution)/shard_map/all_to_all | solution.py:149
  26.3 0.8 copy.149
  27.1 0.7 gather_fusion.5
  27.8 0.9 fusion.42
  28.6 1.0 copy.147
  29.6 1.0 gather_fusion.3
  30.6 3.7 %all-to-all-done.2 = s32[64,1,1]{2,1,0:T(1,128)S(1)} async-done(((s32[64,1,1]{2,1,0:T(1,128)}), s32[64,1,1]{2,1,0:T(1,128)S(1)}, u32[]{:S(2)}, u32[]{:S(2)}) %all-to-all-start.2) | async-done | bytes 288 | tf_op jit(solution)/shard_map/all_to_all | solution.py:149
  34.3 9.0 %all-to-all-start.5 = ((bf16[64,3,1,256]{3,1,2,0:T(4,128)(2,1)}), bf16[64,3,1,256]{3,1,2,0:T(4,128)(2,1)S(1)}, u32[]{:S(2)}, u32[]{:S(2)}) async-start(bf16[64,3,1,256]{3,1,2,0:T(4,128)(2,1)} %fusion.42), calls=%async_computation.5 | async-start | bytes 262144 | tf_op jit(solution)/shard_map/all_to_all | solution.py:164
  43.3 1.2 fusion.16
  44.5 7.9 %all-to-all-done.5 = bf16[64,3,1,256]{3,1,2,0:T(4,128)(2,1)S(1)} async-done(((bf16[64,3,1,256]{3,1,2,0:T(4,128)(2,1)}), bf16[64,3,1,256]{3,1,2,0:T(4,128)(2,1)S(1)}, u32[]{:S(2)}, u32[]{:S(2)}) %all-to-all-start.5) | async-done | bytes 98336 | tf_op jit(solution)/shard_map/all_to_all | solution.py:164
  52.5 8.3 %all-to-all-start.3 = ((bf16[64,3,1,1024]{3,1,2,0:T(4,128)(2,1)}), bf16[64,3,1,1024]{3,1,2,0:T(4,128)(2,1)S(1)}, u32[]{:S(2)}, u32[]{:S(2)}) async-start(bf16[64,3,1,1024]{3,1,2,0:T(4,128)(2,1)} %fusion.16), calls=%async_computation.3 | async-start | bytes 1048576 | tf_op jit(solution)/shard_map/all_to_all | solution.py:161
  60.7 1.6 gather_fusion.4
  62.3 1.0 fusion.14
  63.3 13.1 %all-to-all-done.3 = bf16[64,3,1,1024]{3,1,2,0:T(4,128)(2,1)S(1)} async-done(((bf16[64,3,1,1024]{3,1,2,0:T(4,128)(2,1)}), bf16[64,3,1,1024]{3,1,2,0:T(4,128)(2,1)S(1)}, u32[]{:S(2)}, u32[]{:S(2)}) %all-to-all-start.3) | async-done | bytes 393248 | tf_op jit(solution)/shard_map/all_to_all | solution.py:161
  76.4 7.3 %all-to-all-start.4 = ((bf16[64,16,1,256]{3,1,2,0:T(8,128)(2,1)}), bf16[64,16,1,256]{3,1,2,0:T(8,128)(2,1)S(1)}, u32[]{:S(2)}, u32[]{:S(2)}) async-start(bf16[64,16,1,256]{3,1,2,0:T(8,128)(2,1)} %fusion.14), calls=%async_computation.4 | async-start | bytes 1048576 | tf_op jit(solution)/shard_map/all_to_all | solution.py:167
  83.7 3.0 %gather_fusion = bf16[64,3,2,1024]{3,2,1,0:T(2,128)(2,1)} fusion(bf16[16,3,2,1024]{3,2,1,0:T(2,128)(2,1)S(1)} %copy-done.5, s32[1024]{0:T(1024)S(1)} %pad_clamp_fusion), kind=kCustom, calls=%fused_computation | custom fusion | bytes 1573120 | tf_op jit(solution)/shard_map/jit(_take)/gather | solution.py:8
  86.7 3.1 %broadcast_select_fusion.1 = bf16[64,3,2,1024]{3,2,1,0:T(2,128)(2,1)} fusion(pred[64]{0:T(512)(128)(4,1)S(1)} %fusion.73, bf16[64,3,2,1024]{3,2,1,0:T(2,128)(2,1)} %gather_fusion, pred[64]{0:T(512)(128)(4,1)S(1)} %compare_and_fusion), kind=kLoop, calls=%fused_computation.22 | loop fusion | flops 786432 | bytes 1572992 | tf_op jit(solution)/shard_map/jit(_where)/select_n | solution.py:10
  89.7 9.0 %all-to-all-done.4 = bf16[64,16,1,256]{3,1,2,0:T(8,128)(2,1)S(1)} async-done(((bf16[64,16,1,256]{3,1,2,0:T(8,128)(2,1)}), bf16[64,16,1,256]{3,1,2,0:T(8,128)(2,1)S(1)}, u32[]{:S(2)}, u32[]{:S(2)}) %all-to-all-start.4) | async-done | bytes 524320 | tf_op jit(solution)/shard_map/all_to_all | solution.py:167
  98.7 7.3 %all-to-all-start = ((bf16[64,3,2,1024]{3,2,1,0:T(2,128)(2,1)}), bf16[64,3,2,1024]{3,2,1,0:T(2,128)(2,1)S(1)}, u32[]{:S(2)}, u32[]{:S(2)}) async-start(bf16[64,3,2,1024]{3,2,1,0:T(2,128)(2,1)} %broadcast_select_fusion.1), calls=%async_computation | async-start | bytes 1572864 | tf_op jit(solution)/shard_map/all_to_all | solution.py:154
  106.0 2.8 gather_fusion.1
  108.9 4.7 %select_select_fusion = f32[64,16,1024]{2,1,0:T(8,128)} fusion(f32[64,16,1024]{2,1,0:T(8,128)} %gather_fusion.1, pred[64]{0:T(512)(128)(4,1)S(1)} %compare_and_fusion, pred[64]{0:T(512)(128)(4,1)S(1)} %fusion.73), kind=kLoop, calls=%fused_computation.9 | loop fusion | flops 2097152 | bytes 8388736 | tf_op jit(solution)/shard_map/jit(_where)/select_n | solution.py:10
  113.6 12.3 %all-to-all-done = bf16[64,3,2,1024]{3,2,1,0:T(2,128)(2,1)S(1)} async-done(((bf16[64,3,2,1024]{3,2,1,0:T(2,128)(2,1)}), bf16[64,3,2,1024]{3,2,1,0:T(2,128)(2,1)S(1)}, u32[]{:S(2)}, u32[]{:S(2)}) %all-to-all-start) | async-done | bytes 786464 | tf_op jit(solution)/shard_map/all_to_all | solution.py:154
  125.9 7.8 %all-to-all-start.1 = ((f32[64,16,1024]{2,1,0:T(8,128)}), f32[64,16,1024]{2,1,0:T(8,128)}, u32[]{:S(2)}, u32[]{:S(2)}) async-start(f32[64,16,1024]{2,1,0:T(8,128)} %select_select_fusion), calls=%async_computation.1 | async-start | bytes 8388608 | tf_op jit(solution)/shard_map/all_to_all | solution.py:142
  133.9 0.6 exponential_negate_fusion
  134.6 1.2 reduce.24
  136.2 1.6 slice_reduce_fusion.2
  138.2 0.2 select_reduce_fusion.4
  138.7 0.3 select_reduce_fusion.2
  139.1 0.2 convolution_multiply_fusion
  139.3 0.4 fusion.35
  139.9 0.4 fusion.36
  140.7 0.3 fusion.38
  141.0 1.0 fusion.13
  142.0 0.3 fusion.39
  142.3 1.0 fusion.12
  143.3 1.0 fusion.40
  144.3 0.9 select_select_fusion.1
  145.3 2.0 fusion.86
  147.3 1.2 fusion.84
  148.4 1.1 fusion.83
  149.6 1.2 fusion.82
  150.8 2.1 fusion.11
  152.8 1.6 convert_element_type.138
  154.4 1.6 convert_element_type.134
  156.1 1.6 convert_element_type.130
  157.7 1.0 copy.81
  158.7 1.8 pad_maximum_fusion.1
  160.5 64.9 %all-reduce.4.cloned.1.call-done = (f32[64,544]{1,0:T(8,128)}, f32[64,544]{1,0:T(8,128)}, f32[64,544]{1,0:T(8,128)}) async-done(((f32[64,544]{1,0:T(8,128)}, f32[64,544]{1,0:T(8,128)}, f32[64,544]{1,0:T(8,128)}), (f32[64,544]{1,0:T(8,128)}, f32[64,544]{1,0:T(8,128)}, f32[64,544]{1,0:T(8,128)})) %all-reduce.4.cloned.1.call-update) | async-done | bytes 417808 | tf_op jit(solution)/shard_map/psum | solution.py:60
  225.4 1.5 fusion.89
  226.9 1.6 fusion.87
  228.5 1.4 convert_multiply_fusion.8
  229.9 2.0 convert_multiply_fusion.6
  231.9 2.2 convert_multiply_fusion.4
  234.1 21.0 %all-to-all-done.1 = f32[64,16,1024]{2,1,0:T(8,128)} async-done(((f32[64,16,1024]{2,1,0:T(8,128)}), f32[64,16,1024]{2,1,0:T(8,128)}, u32[]{:S(2)}, u32[]{:S(2)}) %all-to-all-start.1) | async-done | bytes 4194336 | tf_op jit(solution)/shard_map/all_to_all | solution.py:142
  255.1 5.4 %fusion = f32[64,1,1024]{2,1,0:T(1,128)S(1)} fusion(f32[64,16,1]{1,2,0:T(1,128)} %bitcast.197, f32[64,16,1024]{2,1,0:T(8,128)} %all-to-all-done.1, f32[64,1024]{1,0:T(8,128)S(1)} %get-tuple-element.59, f32[64,16]{1,0:T(8,128)} %get-tuple-element.46, f32[16,1024]{1,0:T(8,128)S(1)} %copy-done.20, f32[64,1024]{1,0:T(8,128)S(1)} %get-tuple-element.60), kind=kOutput, calls=%fused_computation.10 | convolution fusion | flops 16777216 | bytes 5054464 | tf_op jit(solution)/shard_map/nsc,ns->nc/dot_general | solution.py:73
  260.5 6.2 %fusion.85 = f32[64,1,1024]{2,1,0:T(1,128)S(1)} fusion(f32[64,16,1]{1,2,0:T(1,128)S(1)} %bitcast.196, f32[64,16,1024]{2,1,0:T(8,128)} %all-to-all-done.1, f32[64,1024]{1,0:T(8,128)S(1)} %get-tuple-element.61, f32[64,16]{1,0:T(8,128)S(1)} %copy-done.24, f32[64,1024]{1,0:T(8,128)S(1)} %copy-done.12, f32[64,1024]{1,0:T(8,128)S(1)} %get-tuple-element.59, ...), kind=kOutput, calls=%fused_computation.191 | convolution fusion | flops 20971520 | bytes 5582848 | tf_op jit(solution)/shard_map/nsc,ns->nc/dot_general | solution.py:73
  266.9 7.0 %fusion.2 = f32[64,1,1024]{2,1,0:T(1,128)S(1)} fusion(f32[64,16,1]{1,2,0:T(1,128)S(1)} %bitcast.195, f32[64,1024]{1,0:T(8,128)S(1)} %copy-done.13, f32[64,16]{1,0:T(8,128)S(1)} %copy-done.21, f32[64,1024]{1,0:T(8,128)S(1)} %copy-done.14, f32[16,1024]{1,0:T(8,128)S(1)} %copy-done.20, f32[64,16,1024]{2,1,0:T(8,128)} %all-to-all-done.1, ...), kind=kOutput, calls=%fused_computation.12 | convolution fusion | flops 25165824 | bytes 6111232 | tf_op jit(solution)/shard_map/nsc,ns->nc/dot_general | solution.py:73
  274.0 0.6 fusion.57
  274.6 0.8 pad_maximum_fusion
  275.4 6.1 %fusion.1 = bf16[64,16,1024]{2,1,0:T(8,128)(2,1)} fusion(f32[64,1024]{1,0:T(8,128)S(1)} %copy-done.13, f32[64,16]{1,0:T(8,128)S(1)} %copy-done.21, f32[64,1024]{1,0:T(8,128)S(1)} %copy-done.14, f32[16,1024]{1,0:T(8,128)S(1)} %copy-done.20, f32[64,1024]{1,0:T(8,128)S(1)} %copy-done.11, f32[64,16]{1,0:T(8,128)S(1)} %copy-done.25, ...), kind=kLoop, calls=%fused_computation.11 | loop fusion | flops 13631488 | bytes 7942144 | tf_op jit(solution)/shard_map/convert_element_type | solution.py:109
  (96 shorter events, 2.1 us)
Async XLA Ops:
  7.2 140.1 %copy-start = (bf16[1024,544]{0,1:T(8,128)(2,1)S(1)}, bf16[1024,544]{0,1:T(8,128)(2,1)}, u32[]{:S(2)}) copy-start(bf16[1024,544]{0,1:T(8,128)(2,1)} %param.19) | copy-start | bytes 3342340
  7.2 76.5 %copy-start.5 = (bf16[16,3,2,1024]{3,2,1,0:T(2,128)(2,1)S(1)}, bf16[16,3,2,1024]{3,2,1,0:T(2,128)(2,1)}, u32[]{:S(2)}) copy-start(bf16[16,3,2,1024]{3,2,1,0:T(2,128)(2,1)} %param.12) | copy-start | bytes 589828
  11.2 23.1 %all-to-all-start.2 = ((s32[64,1,1]{2,1,0:T(1,128)}), s32[64,1,1]{2,1,0:T(1,128)S(1)}, u32[]{:S(2)}, u32[]{:S(2)}) async-start(s32[64,1,1]{2,1,0:T(1,128)} %copy.69), calls=%async_computation.2 | async-start | bytes 65536 | tf_op jit(solution)/shard_map/all_to_all | solution.py:149
  34.3 18.2 %all-to-all-start.5 = ((bf16[64,3,1,256]{3,1,2,0:T(4,128)(2,1)}), bf16[64,3,1,256]{3,1,2,0:T(4,128)(2,1)S(1)}, u32[]{:S(2)}, u32[]{:S(2)}) async-start(bf16[64,3,1,256]{3,1,2,0:T(4,128)(2,1)} %fusion.42), calls=%async_computation.5 | async-start | bytes 262144 | tf_op jit(solution)/shard_map/all_to_all | solution.py:164
  52.4 8.3 %copy-start.18 = (bf16[64,3,1,256]{3,1,2,0:T(4,128)(2,1)}, bf16[64,3,1,256]{3,1,2,0:T(4,128)(2,1)S(1)}, u32[]{:S(2)}) copy-start(bf16[64,3,1,256]{3,1,2,0:T(4,128)(2,1)S(1)} %all-to-all-done.5) | copy-start | bytes 294916
  52.5 23.9 %all-to-all-start.3 = ((bf16[64,3,1,1024]{3,1,2,0:T(4,128)(2,1)}), bf16[64,3,1,1024]{3,1,2,0:T(4,128)(2,1)S(1)}, u32[]{:S(2)}, u32[]{:S(2)}) async-start(bf16[64,3,1,1024]{3,1,2,0:T(4,128)(2,1)} %fusion.16), calls=%async_computation.3 | async-start | bytes 1048576 | tf_op jit(solution)/shard_map/all_to_all | solution.py:161
  60.7 45.3 %copy-start.1 = (f32[16,16,1024]{2,1,0:T(8,128)S(1)}, f32[16,16,1024]{2,1,0:T(8,128)}, u32[]{:S(2)}) copy-start(f32[16,16,1024]{2,1,0:T(8,128)} %param.15) | copy-start | bytes 3145732
  76.4 22.3 %copy-start.3 = (bf16[64,3,1,1024]{3,1,2,0:T(4,128)(2,1)}, bf16[64,3,1,1024]{3,1,2,0:T(4,128)(2,1)S(1)}, u32[]{:S(2)}) copy-start(bf16[64,3,1,1024]{3,1,2,0:T(4,128)(2,1)S(1)} %all-to-all-done.3) | copy-start | bytes 1179652
  76.4 22.3 %all-to-all-start.4 = ((bf16[64,16,1,256]{3,1,2,0:T(8,128)(2,1)}), bf16[64,16,1,256]{3,1,2,0:T(8,128)(2,1)S(1)}, u32[]{:S(2)}, u32[]{:S(2)}) async-start(bf16[64,16,1,256]{3,1,2,0:T(8,128)(2,1)} %fusion.14), calls=%async_computation.4 | async-start | bytes 1048576 | tf_op jit(solution)/shard_map/all_to_all | solution.py:167
  98.7 27.2 %all-to-all-start = ((bf16[64,3,2,1024]{3,2,1,0:T(2,128)(2,1)}), bf16[64,3,2,1024]{3,2,1,0:T(2,128)(2,1)S(1)}, u32[]{:S(2)}, u32[]{:S(2)}) async-start(bf16[64,3,2,1024]{3,2,1,0:T(2,128)(2,1)} %broadcast_select_fusion.1), calls=%async_computation | async-start | bytes 1572864 | tf_op jit(solution)/shard_map/all_to_all | solution.py:154
  113.6 20.3 %copy-start.27 = (f32[16,1024]{1,0:T(8,128)S(1)}, f32[16,1024]{1,0:T(8,128)}, u32[]{:S(2)}) copy-start(f32[16,1024]{1,0:T(8,128)} %param.22) | copy-start | bytes 196612
  113.6 22.5 %copy-start.19 = (bf16[64,3,1,256]{3,1,2,0:T(4,128)(2,1)S(1)}, bf16[64,3,1,256]{3,1,2,0:T(4,128)(2,1)}, u32[]{:S(2)}) copy-start(bf16[64,3,1,256]{3,1,2,0:T(4,128)(2,1)} %copy-done.18) | copy-start | bytes 294916
  113.6 22.6 %copy-start.4 = (bf16[64,3,1,1024]{3,1,2,0:T(4,128)(2,1)S(1)}, bf16[64,3,1,1024]{3,1,2,0:T(4,128)(2,1)}, u32[]{:S(2)}) copy-start(bf16[64,3,1,1024]{3,1,2,0:T(4,128)(2,1)} %copy-done.3) | copy-start | bytes 1179652
  125.9 129.2 %all-to-all-start.1 = ((f32[64,16,1024]{2,1,0:T(8,128)}), f32[64,16,1024]{2,1,0:T(8,128)}, u32[]{:S(2)}, u32[]{:S(2)}) async-start(f32[64,16,1024]{2,1,0:T(8,128)} %select_select_fusion), calls=%async_computation.1 | async-start | bytes 8388608 | tf_op jit(solution)/shard_map/all_to_all | solution.py:142
  133.6 91.7 %all-reduce.4.cloned.1.call-start = ((), (), s32[]{:S(2)}) async-start(), calls=%async_computation.6 | async-start | bytes 983040 | tf_op jit(solution)/shard_map/psum | solution.py:60
  138.2 3.8 %copy-start.26 = (f32[64,8,3]{1,2,0:T(4,128)}, f32[64,8,3]{1,2,0:T(4,128)S(1)}, u32[]{:S(2)}) copy-start(f32[64,8,3]{1,2,0:T(4,128)S(1)} %get-tuple-element.68) | copy-start | bytes 18436
  147.3 1.2 copy-start.6
  147.3 2.3 copy-start.8
  148.4 80.0 %copy-start.2 = (bf16[512,1024]{1,0:T(8,128)(2,1)S(1)}, bf16[512,1024]{1,0:T(8,128)(2,1)}, u32[]{:S(2)}) copy-start(bf16[512,1024]{1,0:T(8,128)(2,1)} %param.20) | copy-start | bytes 3145732
  148.4 80.0 %copy-start.28 = (f32[1024]{0:T(1024)S(1)}, f32[1024]{0:T(1024)}, u32[]{:S(2)}) copy-start(f32[1024]{0:T(1024)} %param.21) | copy-start | bytes 12292
  149.6 80.3 %copy-start.7 = (bf16[64,1,1,1024]{3,2,1,0:T(2,128)(2,1)S(1)}, bf16[64,1,1,1024]{3,2,1,0:T(2,128)(2,1)}, u32[]{:S(2)}) copy-start(bf16[64,1,1,1024]{3,2,1,0:T(2,128)(2,1)} %copy-done.6) | copy-start | bytes 393220
  156.0 99.0 %copy-start.20 = (f32[16,1024]{1,0:T(8,128)S(1)}, f32[16,1024]{1,0:T(8,128)}, u32[]{:S(2)}) copy-start(f32[16,1024]{1,0:T(8,128)} %exponential_negate_fusion) | copy-start | bytes 196612
  231.9 34.9 %copy-start.10 = (f32[64,1024]{1,0:T(8,128)}, f32[64,1024]{1,0:T(8,128)S(1)}, u32[]{:S(2)}) copy-start(f32[64,1024]{1,0:T(8,128)S(1)} %get-tuple-element.61) | copy-start | bytes 786436
  234.1 26.4 %copy-start.12 = (f32[64,1024]{1,0:T(8,128)S(1)}, f32[64,1024]{1,0:T(8,128)}, u32[]{:S(2)}) copy-start(f32[64,1024]{1,0:T(8,128)} %get-tuple-element.62) | copy-start | bytes 786436
  234.1 26.4 %copy-start.22 = (f32[64,16]{1,0:T(8,128)S(1)}, f32[64,16]{1,0:T(8,128)}, u32[]{:S(2)}) copy-start(f32[64,16]{1,0:T(8,128)} %get-tuple-element.46) | copy-start | bytes 12292
  234.1 26.4 %copy-start.24 = (f32[64,16]{1,0:T(8,128)S(1)}, f32[64,16]{1,0:T(8,128)}, u32[]{:S(2)}) copy-start(f32[64,16]{1,0:T(8,128)} %get-tuple-element.74) | copy-start | bytes 12292
  234.1 26.4 %copy-start.30 = (f32[64,16]{1,0:T(8,128)S(1)}, f32[64,16]{1,0:T(8,128)}, u32[]{:S(2)}) copy-start(f32[64,16]{1,0:T(8,128)} %get-tuple-element.75) | copy-start | bytes 12292
  260.5 6.3 %copy-start.13 = (f32[64,1024]{1,0:T(8,128)S(1)}, f32[64,1024]{1,0:T(8,128)}, u32[]{:S(2)}) copy-start(f32[64,1024]{1,0:T(8,128)} %get-tuple-element.63) | copy-start | bytes 786436
  260.5 6.3 %copy-start.14 = (f32[64,1024]{1,0:T(8,128)S(1)}, f32[64,1024]{1,0:T(8,128)}, u32[]{:S(2)}) copy-start(f32[64,1024]{1,0:T(8,128)} %get-tuple-element.64) | copy-start | bytes 786436
  260.5 6.3 %copy-start.21 = (f32[64,16]{1,0:T(8,128)S(1)}, f32[64,16]{1,0:T(8,128)}, u32[]{:S(2)}) copy-start(f32[64,16]{1,0:T(8,128)} %get-tuple-element.49) | copy-start | bytes 12292
  260.5 6.3 %copy-start.23 = (f32[64,16]{1,0:T(8,128)S(1)}, f32[64,16]{1,0:T(8,128)}, u32[]{:S(2)}) copy-start(f32[64,16]{1,0:T(8,128)} %get-tuple-element.46) | copy-start | bytes 12292
  260.5 6.3 %copy-start.25 = (f32[64,16]{1,0:T(8,128)S(1)}, f32[64,16]{1,0:T(8,128)}, u32[]{:S(2)}) copy-start(f32[64,16]{1,0:T(8,128)} %get-tuple-element.74) | copy-start | bytes 12292
  260.5 6.3 %copy-start.29 = (f32[64,16]{1,0:T(8,128)S(1)}, f32[64,16]{1,0:T(8,128)}, u32[]{:S(2)}) copy-start(f32[64,16]{1,0:T(8,128)} %get-tuple-element.50) | copy-start | bytes 12292
  266.8 7.1 %copy-start.9 = (bf16[64,1,1,1024]{3,2,1,0:T(2,128)(2,1)S(1)}, bf16[64,1,1,1024]{3,2,1,0:T(2,128)(2,1)}, u32[]{:S(2)}) copy-start(bf16[64,1,1,1024]{3,2,1,0:T(2,128)(2,1)} %copy-done.8) | copy-start | bytes 393220
  266.8 7.1 %copy-start.15 = (bf16[64,1,1,1024]{3,2,1,0:T(2,128)(2,1)S(1)}, bf16[64,1,1,1024]{3,2,1,0:T(2,128)(2,1)}, u32[]{:S(2)}) copy-start(bf16[64,1,1,1024]{3,2,1,0:T(2,128)(2,1)} %get-tuple-element.39) | copy-start | bytes 393220
  266.9 7.1 %copy-start.16 = (bf16[64,1,1,1024]{3,2,1,0:T(2,128)(2,1)S(1)}, bf16[64,1,1,1024]{3,2,1,0:T(2,128)(2,1)}, u32[]{:S(2)}) copy-start(bf16[64,1,1,1024]{3,2,1,0:T(2,128)(2,1)} %get-tuple-element.41) | copy-start | bytes 393220
  266.9 7.1 %copy-start.17 = (bf16[64,1,1,1024]{3,2,1,0:T(2,128)(2,1)S(1)}, bf16[64,1,1,1024]{3,2,1,0:T(2,128)(2,1)}, u32[]{:S(2)}) copy-start(bf16[64,1,1,1024]{3,2,1,0:T(2,128)(2,1)} %get-tuple-element.44) | copy-start | bytes 393220
  266.9 7.1 %copy-start.31 = (f32[1024]{0:T(1024)S(1)}, f32[1024]{0:T(1024)}, u32[]{:S(2)}) copy-start(f32[1024]{0:T(1024)} %param.23) | copy-start | bytes 12292
  266.9 8.5 %copy-start.11 = (f32[64,1024]{1,0:T(8,128)S(1)}, f32[64,1024]{1,0:T(8,128)}, u32[]{:S(2)}) copy-start(f32[64,1024]{1,0:T(8,128)} %copy-done.10) | copy-start | bytes 786436
Sparse Core Ops, SparseCore 0:
  150.9 74.4 all-reduce.3
where the time goes:
time: 289 us; the launch traced here: 288 us
  waiting for transfers between devices  132 us (46%)
  starting transfers between devices  55 us (19%)
  matrix products  35.1 us (12%)
  other arithmetic  25.9 us (9%)
  local copies, waits for them, and re-layouts  25.8 us (9%)
  between operations  14.7 us (5%)
    psum x1, waiting for transfers between devices, decode(): lax.psum(jnp.dot(x_in, xproj_w, preferred_element_type=jnp.float32), 'ten...  64.9 us
    all_to_all x1, waiting for transfers between devices, per_device(): lax.all_to_all(place_rows(ssm_state, chosen, present), 'replica', split_a...  21 us
    dot_general x3, matrix products, decode(): jnp.einsum('nsc,ns->nc', ssm_carry, c_vector, precision=lax.Precision.HIG...  18.6 us
    all_to_all x1, starting transfers between devices, per_device(): lax.all_to_all(place_rows(lengths, chosen, present), 'replica', split_axi...  15.1 us
    all_to_all x1, waiting for transfers between devices, per_device(): lax.all_to_all(place_rows(queries, chosen, present), 'replica', split_axi...  13.1 us
    all_to_all x1, waiting for transfers between devices, per_device(): lax.all_to_all(place_rows(mamba_in, chosen, present), 'replica', split_ax...  12.3 us
    select_n x6, other arithmetic, place_rows(): return jnp.where(keeper, gathered, jnp.zeros_like(gathered))  10.8 us
    gather x6, local copies, waits for them, and re-layouts, place_rows(): gathered = jnp.take(source_rows, chosen, axis=0)  10.5 us
  transfers between devices with their start and end apart: 7, of which 7 were waited for; matrix products, arithmetic and copies ran while one was open for 20% of the time, Pallas kernels for 0%

commit v1 on v0

v1 whole, which is shorter than its diff:
```python
import jax
import jax.numpy as jnp
from jax import lax
from jax.sharding import PartitionSpec as P


def place_rows(source_rows, chosen, present):
    gathered = jnp.take(source_rows, chosen, axis=0)
    keeper = present.reshape((present.shape[0],) + (1,) * (source_rows.ndim - 1))
    return jnp.where(keeper, gathered, jnp.zeros_like(gathered))


def extend_pages(kv_pages, new_kv, lengths):
    row_count = kv_pages.shape[0]
    step_count = new_kv.shape[1]
    padding = jnp.zeros((row_count, step_count) + kv_pages.shape[2:], kv_pages.dtype)
    grown = jnp.concatenate([kv_pages, padding], axis=1)
    position = jnp.arange(grown.shape[1], dtype=jnp.int32)[None, :]
    for offset in range(step_count):
        hit = (position == lengths[:, None] + offset)[:, :, None, None]
        grown = jnp.where(hit, new_kv[:, offset][:, None], grown)
    return grown


def sending_rows(destination, peer_count):
    row_count = destination.shape[0]
    capacity = (row_count + peer_count - 1) // peer_count
    targets = destination[:, 0]
    row_ids = jnp.arange(row_count, dtype=jnp.int32)
    earlier = row_ids[None, :] < row_ids[:, None]
    same = targets[:, None] == targets[None, :]
    rank = jnp.sum((same & earlier).astype(jnp.int32), axis=1)
    send_slot = targets * capacity + rank
    slot_ids = jnp.arange(peer_count * capacity, dtype=jnp.int32)
    matches = send_slot[None, :] == slot_ids[:, None]
    return jnp.sum(jnp.where(matches, row_ids[None, :], 0), axis=1), jnp.any(matches, axis=1)


def attend(queries, new_kv, kv_cache, lengths):
    rows, steps, _, query_width = queries.shape
    context = kv_cache.shape[1]
    width = kv_cache.shape[3] // 2
    group = query_width // width
    query = queries.reshape(rows, steps * group, width)
    pages = jnp.concatenate([kv_cache[:, :, 0], new_kv[:, :, 0]], axis=1)
    scores = jnp.einsum(
        "nqd,nkd->nqk", query, pages[..., :width], preferred_element_type=jnp.float32
    ) * (width ** (-0.5))
    key_id = jnp.arange(context + steps, dtype=jnp.int32)
    step_id = jnp.arange(steps * group, dtype=jnp.int32) // group
    live = jnp.where(
        (key_id < context)[None, None, :],
        key_id[None, None, :] < lengths[:, None, None],
        (key_id[None, :] - context <= step_id[:, None])[None],
    )
    top = jnp.max(jnp.where(live, scores, -1e30), axis=-1, keepdims=True)
    raised = jnp.where(live, jnp.exp(scores - top), 0.0)
    weights = (raised / jnp.sum(raised, axis=-1, keepdims=True)).astype(jnp.bfloat16)
    summed = jnp.einsum(
        "nqk,nkd->nqd", weights, pages[..., width:], preferred_element_type=jnp.float32
    )
    return summed.astype(jnp.bfloat16).reshape(rows, steps, query_width)


def scan_state(mamba_in, ssm_state, xproj_w, dtproj_w, dt_bias, a_log, d_skip):
    rows, steps, _, width = mamba_in.shape
    low_width = dtproj_w.shape[0]
    state_size = a_log.shape[0]
    x_in = mamba_in[:, :, 0].reshape(rows * steps, width)
    projected = lax.psum(jnp.dot(x_in, xproj_w, preferred_element_type=jnp.float32), "tensor")
    low_rank = projected[:, :low_width].astype(jnp.bfloat16)
    step_size = jax.nn.softplus(
        jnp.dot(low_rank, dtproj_w, preferred_element_type=jnp.float32) + dt_bias
    ).reshape(rows, steps, width)
    b_all = projected[:, low_width : low_width + state_size].reshape(rows, steps, state_size)
    c_all = projected[:, low_width + state_size :].reshape(rows, steps, state_size)
    decay_rate = -jnp.exp(a_log)
    carry = ssm_state
    mixed = []
    for step in range(steps):
        x_float = mamba_in[:, step, 0].astype(jnp.float32)
        z_float = mamba_in[:, step, 1].astype(jnp.float32)
        size = step_size[:, step]
        carry = (
            jnp.exp(size[:, None, :] * decay_rate[None]) * carry
            + b_all[:, step, :, None] * (size * x_float)[:, None, :]
        )
        readout = jnp.sum(carry * c_all[:, step, :, None], axis=1) + d_skip * x_float
        mixed.append((readout * jax.nn.silu(z_float)).astype(jnp.bfloat16))
    return jnp.stack(mixed, axis=1), carry.astype(jnp.bfloat16)


def exchange(rows):
    return lax.all_to_all(rows, "replica", split_axis=0, concat_axis=0, tiled=True)


def per_device(
    mamba_in,
    queries,
    new_kv,
    ssm_state,
    kv_cache,
    lengths,
    destination,
    xproj_w,
    dtproj_w,
    dt_bias,
    a_log,
    d_skip,
):
    chosen, present = sending_rows(destination, lax.axis_size("replica"))
    rows, steps, _, width = mamba_in.shape
    state_size = a_log.shape[0]
    slots = chosen.shape[0]
    attended = attend(queries, new_kv, kv_cache, lengths)
    grown = extend_pages(kv_cache, new_kv, lengths)
    query_width = queries.shape[3]
    attended_size = steps * query_width
    early = jnp.concatenate(
        [attended.reshape(rows, attended_size), grown.reshape(rows, -1)], axis=1
    ).reshape(rows, 16, -1)
    early = exchange(place_rows(early, chosen, present)).reshape(slots, -1)
    mixed, state = scan_state(mamba_in, ssm_state, xproj_w, dtproj_w, dt_bias, a_log, d_skip)
    late = jnp.concatenate([state, mixed.reshape(rows, state_size, -1)], axis=2)
    late = exchange(place_rows(late, chosen, present))
    return (
        late[:, :, width:].reshape(slots, steps, width),
        early[:, :attended_size].reshape(slots, steps, 1, query_width),
        late[:, :, :width],
        early[:, attended_size:].reshape((slots,) + grown.shape[1:]),
    )


def solution(mesh):
    placed = (
        P("replica", None, None, "tensor"),
        P("replica", None, "tensor", None),
        P("replica", None, "tensor", None),
        P("replica", None, "tensor"),
        P("replica", None, "tensor", None),
        P("replica"),
        P("replica", None),
        P("tensor", None),
        P(None, "tensor"),
        P("tensor"),
        P(None, "tensor"),
        P("tensor"),
    )
    return jax.shard_map(
        per_device,
        mesh=mesh,
        in_specs=placed,
        out_specs=(
            P("replica", None, "tensor"),
            P("replica", None, "tensor", None),
            P("replica", None, "tensor"),
            P("replica", None, "tensor", None),
        ),
        check_vma=False,
    )
```

time: 289 us -> 201 us (0.70)
  the two profiles are of different devices: /device:TPU:112 before, /device:TPU:101 now
where the time goes in v1:
time: 201 us; the launch traced here: 200 us
  waiting for transfers between devices  115 us (57%)
  starting transfers between devices  27.6 us (14%)
  local copies, waits for them, and re-layouts  24.9 us (12%)
  other arithmetic  14.6 us (7%)
  between operations  14.4 us (7%)
  matrix products  3.6 us (2%)
    all_to_all x2, waiting for transfers between devices, exchange(): lax.all_to_all(rows, 'replica', split_axis=0, concat_axis=0, tiled=True)  70.5 us
    psum x1, waiting for transfers between devices, scan_state(): lax.psum(jnp.dot(x_in, xproj_w, preferred_element_type=jnp.float32), 'ten...  44.9 us
    all_to_all x2, starting transfers between devices, exchange(): lax.all_to_all(rows, 'replica', split_axis=0, concat_axis=0, tiled=True)  27.5 us
    select_n x2, other arithmetic, place_rows(): return jnp.where(keeper, gathered, jnp.zeros_like(gathered))  4.83 us
    unnamed x29, local copies, waits for them, and re-layouts  4.61 us
  transfers between devices with their start and end apart: 3, of which 2 were waited for; matrix products, arithmetic and copies ran while one was open for 17% of the time, Pallas kernels for 0%

profile of v1, /device:TPU:101, one launch (start us, length us, event | category | flops | bytes accessed | tf_op | source)
XLA Modules:
  0.0 200.4 jit_solution(8717174642472078301)
XLA Ops:
  7.2 0.0 copy-start
  7.2 0.0 copy-start.4
  7.2 0.0 all-reduce.3.cloned.1.call-start
  7.2 1.6 slice_reduce_fusion
  8.8 0.1 reshape_squeeze.3
  8.9 1.1 fusion.57
  10.0 0.0 all-reduce.3.cloned.1.call-update
  10.1 0.9 convert_reduce_fusion
  11.0 0.7 bitcast_add_fusion
  11.6 0.1 select_reduce_fusion.1
  11.7 0.1 fusion.41
  11.9 0.7 iota_compare_fusion.3
  12.6 0.7 broadcast_add_fusion.1
  13.3 0.8 copy.121
  14.0 0.7 slice_bitcast_fusion.2
  14.8 1.0 copy.70
  15.8 0.1 reshape.459
  15.8 0.1 broadcast_compare_fusion
  15.9 0.2 fusion.4
  16.1 0.2 fusion.56
  16.3 0.4 convolution_convert_fusion
  16.7 0.1 iota_compare_fusion.1
  16.8 0.2 select_select_fusion.2
  17.1 0.6 reshape.461
  17.7 0.6 gather_fusion.1
  18.3 0.0 copy-done.7
  18.3 0.0 copy-done.9
  18.3 0.0 copy-start.1
  18.3 0.0 copy-start.3
  18.3 0.0 copy-start.6
  18.3 1.2 select_select_fusion.1
  19.5 14.8 %all-to-all-start.1 = ((bf16[64,16,496]{2,1,0:T(8,128)(2,1)}), bf16[64,16,496]{2,1,0:T(8,128)(2,1)S(1)}, u32[]{:S(2)}, u32[]{:S(2)}) async-start(bf16[64,16,496]{2,1,0:T(8,128)(2,1)} %select_select_fusion.1), calls=%async_computation.1 | async-start | bytes 2097152 | tf_op jit(solution)/shard_map/all_to_all | solution.py:94
  34.3 1.0 fusion.52
  35.3 1.5 exponential_negate_fusion
  36.8 44.9 %all-reduce.3.cloned.1.call-done = f32[48,544]{1,0:T(8,128)} async-done(((f32[48,544]{1,0:T(8,128)}), f32[48,544]{1,0:T(8,128)}) %all-reduce.3.cloned.1.call-update) | async-done | bytes 104464 | tf_op jit(solution)/shard_map/psum | solution.py:70
  81.7 1.9 compare_select_fusion
  83.6 1.0 reshape.454
  84.6 0.1 fusion.51
  84.8 0.9 fusion.53
  85.7 0.6 fusion.55
  86.4 0.9 copy_bitcast_fusion.1
  87.3 2.5 %multiply_reduce_fusion.1 = (f32[16,1024]{1,0:T(8,128)S(1)}, f32[16,1024]{1,0:T(8,128)S(1)}, f32[16,1024]{1,0:T(8,128)S(1)}, bf16[16,16,1024]{2,1,0:T(8,128)(2,1)S(1)}) fusion(f32[16,16]{1,0:T(8,128)S(1)} %bitcast.105, f32[16,1024]{1,0:T(8,128)S(1)} %get-tuple-element.57, f32[16,16]{1,0:T(8,128)S(1)} %bitcast.101, f32[16,1024]{1,0:T(8,128)S(1)} %get-tuple-element.40, ...), kind=kLoop, calls=%fused_computation.13 | loop fusion | flops 4931584 | bytes 2234368 | tf_op jit(solution)/shard_map/reduce_sum | solution.py:88
  89.8 1.1 fusion.19
  90.8 0.1 copy.68
  90.9 0.2 reshape.457
  91.1 0.1 pad_maximum_fusion
  91.2 0.0 copy-start.8
  91.2 0.0 copy-start.10
  91.2 2.3 %gather_fusion = bf16[64,16,1216]{2,1,0:T(8,128)(2,1)} fusion(bf16[16,16,1216]{2,1,0:T(8,128)(2,1)S(1)} %pad_maximum_fusion, s32[1024]{0:T(1024)} %copy-done.5), kind=kCustom, calls=%fused_computation | custom fusion | bytes 4980992 | tf_op jit(solution)/shard_map/jit(_take)/gather | solution.py:8
  93.5 3.6 %select_select_fusion = bf16[64,16,1216]{2,1,0:T(8,128)(2,1)} fusion(bf16[64,16,1216]{2,1,0:T(8,128)(2,1)} %gather_fusion, pred[64]{0:T(512)(128)(4,1)S(1)} %copy-done.8, pred[64]{0:T(512)(128)(4,1)S(1)} %copy-done.10), kind=kLoop, calls=%fused_computation.3 | loop fusion | flops 2490368 | bytes 4980864 | tf_op jit(solution)/shard_map/jit(_where)/select_n | solution.py:10
  97.2 0.0 all-to-all-done.1
  97.2 12.7 %all-to-all-start = ((bf16[64,16,1216]{2,1,0:T(8,128)(2,1)}), bf16[64,16,1216]{2,1,0:T(8,128)(2,1)}, u32[]{:S(2)}, u32[]{:S(2)}) async-start(bf16[64,16,1216]{2,1,0:T(8,128)(2,1)} %select_select_fusion), calls=%async_computation | async-start | bytes 5242880 | tf_op jit(solution)/shard_map/all_to_all | solution.py:94
  109.9 1.7 reshape.462
  111.6 0.9 slice.134
  112.5 0.8 slice.132
  113.3 1.5 reshape.464
  114.8 1.0 copy.74
  115.7 0.6 reshape.463
  116.3 0.9 copy.73
  117.2 70.5 %all-to-all-done = bf16[64,16,1216]{2,1,0:T(8,128)(2,1)} async-done(((bf16[64,16,1216]{2,1,0:T(8,128)(2,1)}), bf16[64,16,1216]{2,1,0:T(8,128)(2,1)}, u32[]{:S(2)}, u32[]{:S(2)}) %all-to-all-start) | async-done | bytes 2490400 | tf_op jit(solution)/shard_map/all_to_all | solution.py:94
  187.7 1.1 slice.129
  188.7 0.7 reshape.458
  189.5 0.9 copy.72
  190.4 3.2 %slice.133 = bf16[64,16,1024]{2,1,0:T(8,128)(2,1)} slice(bf16[64,16,1216]{2,1,0:T(8,128)(2,1)} %all-to-all-done), slice={[0:64], [0:16], [0:1024]} | slice | bytes 4194304 | tf_op jit(solution)/shard_map/slice | solution.py:129
  (27 shorter events, 0.2 us)
Async XLA Ops:
  7.2 1.7 copy-start
  7.2 8.7 %copy-start.4 = (bf16[16,16,1,256]{3,1,2,0:T(8,128)(2,1)S(1)}, bf16[16,16,1,256]{3,1,2,0:T(8,128)(2,1)}, u32[]{:S(2)}) copy-start(bf16[16,16,1,256]{3,1,2,0:T(8,128)(2,1)} %param.16) | copy-start | bytes 393220
  7.2 74.5 %all-reduce.3.cloned.1.call-start = ((), (), s32[]{:S(2)}) async-start(), calls=%async_computation.2 | async-start | bytes 245760 | tf_op jit(solution)/shard_map/psum | solution.py:70
  11.7 6.6 %copy-start.7 = (pred[64]{0:T(512)(128)(4,1)}, pred[64]{0:T(512)(128)(4,1)S(1)}, u32[]{:S(2)}) copy-start(pred[64]{0:T(512)(128)(4,1)S(1)} %compare_and_fusion) | copy-start | bytes 196
  11.8 6.5 %copy-start.9 = (pred[64]{0:T(512)(128)(4,1)}, pred[64]{0:T(512)(128)(4,1)S(1)}, u32[]{:S(2)}) copy-start(pred[64]{0:T(512)(128)(4,1)S(1)} %fusion.41) | copy-start | bytes 196
  14.8 2.9 %copy-start.5 = (s32[1024]{0:T(1024)}, s32[1024]{0:T(1024)S(1)}, u32[]{:S(2)}) copy-start(s32[1024]{0:T(1024)S(1)} %pad_clamp_fusion) | copy-start | bytes 12292
  18.3 16.0 %copy-start.1 = (bf16[16,3,2,1024]{3,2,1,0:T(2,128)(2,1)S(1)}, bf16[16,3,2,1024]{3,2,1,0:T(2,128)(2,1)}, u32[]{:S(2)}) copy-start(bf16[16,3,2,1024]{3,2,1,0:T(2,128)(2,1)} %param.12) | copy-start | bytes 589828
  18.3 63.4 %copy-start.3 = (bf16[512,1024]{1,0:T(8,128)(2,1)S(1)}, bf16[512,1024]{1,0:T(8,128)(2,1)}, u32[]{:S(2)}) copy-start(bf16[512,1024]{1,0:T(8,128)(2,1)} %param.20) | copy-start | bytes 3145732
  18.3 63.3 %copy-start.6 = (f32[1024]{0:T(1024)S(1)}, f32[1024]{0:T(1024)}, u32[]{:S(2)}) copy-start(f32[1024]{0:T(1024)} %param.21) | copy-start | bytes 12292
  19.5 77.6 %all-to-all-start.1 = ((bf16[64,16,496]{2,1,0:T(8,128)(2,1)}), bf16[64,16,496]{2,1,0:T(8,128)(2,1)S(1)}, u32[]{:S(2)}, u32[]{:S(2)}) async-start(bf16[64,16,496]{2,1,0:T(8,128)(2,1)} %select_select_fusion.1), calls=%async_computation.1 | async-start | bytes 2097152 | tf_op jit(solution)/shard_map/all_to_all | solution.py:94
  91.2 2.4 %copy-start.8 = (pred[64]{0:T(512)(128)(4,1)S(1)}, pred[64]{0:T(512)(128)(4,1)}, u32[]{:S(2)}) copy-start(pred[64]{0:T(512)(128)(4,1)} %copy-done.7) | copy-start | bytes 196
  91.2 2.4 %copy-start.10 = (pred[64]{0:T(512)(128)(4,1)S(1)}, pred[64]{0:T(512)(128)(4,1)}, u32[]{:S(2)}) copy-start(pred[64]{0:T(512)(128)(4,1)} %copy-done.9) | copy-start | bytes 196
  97.2 90.5 %all-to-all-start = ((bf16[64,16,1216]{2,1,0:T(8,128)(2,1)}), bf16[64,16,1216]{2,1,0:T(8,128)(2,1)}, u32[]{:S(2)}, u32[]{:S(2)}) async-start(bf16[64,16,1216]{2,1,0:T(8,128)(2,1)} %select_select_fusion), calls=%async_computation | async-start | bytes 5242880 | tf_op jit(solution)/shard_map/all_to_all | solution.py:94
  113.3 2.5 %copy-start.2 = (bf16[64,3072]{1,0:T(8,128)(2,1)S(1)}, bf16[64,3072]{1,0:T(8,128)(2,1)}, u32[]{:S(2)}) copy-start(bf16[64,3072]{1,0:T(8,128)(2,1)} %slice.132) | copy-start | bytes 1179652
Sparse Core Ops, SparseCore 0:
  10.9 70.7 all-reduce.2

commit v2 on v1

--- a/solution.py
+++ b/solution.py
@@ -1,13 +1,13 @@
 import jax
 import jax.numpy as jnp
 from jax import lax
+from jax.experimental import pallas as pl
+from jax.experimental.pallas import tpu as pltpu
 from jax.sharding import PartitionSpec as P
 
-
-def place_rows(source_rows, chosen, present):
-    gathered = jnp.take(source_rows, chosen, axis=0)
-    keeper = present.reshape((present.shape[0],) + (1,) * (source_rows.ndim - 1))
-    return jnp.where(keeper, gathered, jnp.zeros_like(gathered))
+MESH = pl.DeviceIdType.MESH
+SIDE = 8
+NEAR_FIRST = (1, 7, 2, 6, 3, 5, 4)
 
 
 def extend_pages(kv_pages, new_kv, lengths):
@@ -90,8 +90,102 @@
     return jnp.stack(mixed, axis=1), carry.astype(jnp.bfloat16)
 
 
-def exchange(rows):
-    return lax.all_to_all(rows, "replica", split_axis=0, concat_axis=0, tiled=True)
+def move_kernel(chosen, rows, out, placed, middle, first_sent, first_come, sent, come):
+    me = lax.axis_index("replica")
+    shard = lax.axis_index("tensor")
+    place = (me // SIDE, me % SIDE)
+
+    def device(route, first, second):
+        return (first * SIDE + second if route == 0 else second * SIDE + first, shard)
+
+    barrier = pltpu.get_barrier_semaphore()
+    for route in range(2):
+        for hop in NEAR_FIRST:
+            peer = device(route, lax.rem(place[route] + hop, SIDE), place[1 - route])
+            pl.semaphore_signal(barrier, inc=1, device_id=peer, device_id_type=MESH)
+
+    def put(index, carry):
+        first, second = index // SIDE, index % SIDE
+        placed[0, first, second] = rows[0, chosen[first * SIDE + second]]
+        placed[1, first, second] = rows[1, chosen[second * SIDE + first]]
+        return carry
+
+    lax.fori_loop(0, SIDE * SIDE, put, 0)
+    pl.semaphore_wait(barrier, 2 * len(NEAR_FIRST))
+
+    first_copies = {}
+    for hop in NEAR_FIRST:
+        for route in range(2):
+            target = lax.rem(place[route] + hop, SIDE)
+            copy = pltpu.make_async_remote_copy(
+                src_ref=placed.at[route, target],
+                dst_ref=middle.at[route, hop],
+                send_sem=first_sent.at[route, hop],
+                recv_sem=first_come.at[route, hop],
+                device_id=device(route, target, place[1 - route]),
+                device_id_type=MESH,
+            )
+            copy.start()
+            first_copies[route, hop] = copy
+
+    def pass_on(route, bundle, origin):
+        mine = place[1 - route]
+
+        def slot(second):
+            pair = (origin, second) if route == 0 else (second, origin)
+            return out.at[route, pair[0], pair[1]]
+
+        for hop in NEAR_FIRST:
+            target = lax.rem(mine + hop, SIDE)
+            pltpu.make_async_remote_copy(
+                src_ref=bundle.at[target],
+                dst_ref=slot(mine),
+                send_sem=sent,
+                recv_sem=come,
+                device_id=device(route, place[route], target),
+                device_id_type=MESH,
+            ).start()
+        slot(mine)[...] = bundle[mine]
+
+    for route in range(2):
+        pass_on(route, placed.at[route, place[route]], place[route])
+    for hop in NEAR_FIRST:
+        for route in range(2):
+            first_copies[route, hop].wait_recv()
+            origin = lax.rem(place[route] + SIDE - hop, SIDE)
+            pass_on(route, middle.at[route, hop], origin)
+    for copy in first_copies.values():
+        copy.wait_send()
+    all_but_own = out.at[:, :, pl.ds(0, SIDE - 1)]
+    pltpu.make_async_copy(all_but_own, all_but_own, sent).wait()
+    pltpu.make_async_copy(all_but_own, all_but_own, come).wait()
+
+
+def move_rows(rows, chosen):
+    tail = rows.shape[2:]
+    whole = (2, SIDE, SIDE) + tail
+    moved = pl.pallas_call(
+        move_kernel,
+        out_shape=jax.ShapeDtypeStruct(whole, rows.dtype),
+        in_specs=[
+            pl.BlockSpec(memory_space=pltpu.SMEM),
+            pl.BlockSpec(memory_space=pltpu.VMEM),
+        ],
+        out_specs=pl.BlockSpec(memory_space=pltpu.VMEM),
+        scratch_shapes=[
+            pltpu.VMEM(whole, rows.dtype),
+            pltpu.VMEM(whole, rows.dtype),
+            pltpu.SemaphoreType.DMA((2, SIDE)),
+            pltpu.SemaphoreType.DMA((2, SIDE)),
+            pltpu.SemaphoreType.DMA,
+            pltpu.SemaphoreType.DMA,
+        ],
+        name="move_rows",
+        compiler_params=pltpu.CompilerParams(
+            collective_id=1, has_side_effects=True, vmem_limit_bytes=32 << 20
+        ),
+    )(chosen, rows)
+    return moved.reshape((2, SIDE * SIDE) + tail)
 
 
 def per_device(
@@ -111,23 +205,31 @@
     chosen, present = sending_rows(destination, lax.axis_size("replica"))
     rows, steps, _, width = mamba_in.shape
     state_size = a_log.shape[0]
-    slots = chosen.shape[0]
+    query_width = queries.shape[3]
+    chosen = jnp.where(present, chosen, rows)
     attended = attend(queries, new_kv, kv_cache, lengths)
     grown = extend_pages(kv_cache, new_kv, lengths)
-    query_width = queries.shape[3]
-    attended_size = steps * query_width
-    early = jnp.concatenate(
-        [attended.reshape(rows, attended_size), grown.reshape(rows, -1)], axis=1
-    ).reshape(rows, 16, -1)
-    early = exchange(place_rows(early, chosen, present)).reshape(slots, -1)
     mixed, state = scan_state(mamba_in, ssm_state, xproj_w, dtproj_w, dt_bias, a_log, d_skip)
-    late = jnp.concatenate([state, mixed.reshape(rows, state_size, -1)], axis=2)
-    late = exchange(place_rows(late, chosen, present))
+    side = jnp.concatenate(
+        [mixed.reshape(rows, -1), attended.reshape(rows, -1), grown.reshape(rows, -1)], axis=1
+    )
+    side_size = side.shape[1]
+    side = side.reshape(rows, state_size, -1)
+    cut = width - 128
+    half = jnp.concatenate([state[:, :, cut:], side], axis=2)
+    half = jnp.pad(half, ((0, 0), (0, 0), (0, cut - half.shape[2])))
+    both = jnp.stack([state[:, :, :cut], half])
+    both = jnp.pad(both, ((0, 0), (0, 1), (0, 0), (0, 0)))
+    main, rest = move_rows(both, chosen)
+    slots = main.shape[0]
+    out_state = jnp.concatenate([main, rest[:, :, :128]], axis=2)
+    rest = rest[:, :, 128 : 128 + side_size // state_size].reshape(slots, side_size)
+    mixed_size, attended_size = steps * width, steps * query_width
     return (
-        late[:, :, width:].reshape(slots, steps, width),
-        early[:, :attended_size].reshape(slots, steps, 1, query_width),
-        late[:, :, :width],
-        early[:, attended_size:].reshape((slots,) + grown.shape[1:]),
+        rest[:, :mixed_size].reshape(slots, steps, width),
+        rest[:, mixed_size : mixed_size + attended_size].reshape(slots, steps, 1, query_width),
+        out_state,
+        rest[:, mixed_size + attended_size :].reshape((slots,) + grown.shape[1:]),
     )
 
 

time: 201 us -> 212 us (1.055)
  the two profiles are of different devices: /device:TPU:101 before, /device:TPU:6 now
where the time goes in v2:
time: 212 us; the launch traced here: 211 us
  Pallas kernels  92.9 us (44%)
  waiting for transfers between devices  68.4 us (32%)
  local copies, waits for them, and re-layouts  25.6 us (12%)
  between operations  14.5 us (7%)
  other arithmetic  6.85 us (3%)
  matrix products  2.93 us (1%)
    pallas_call x1, Pallas kernels, move_rows(): pl.pallas_call(move_kernel, out_shape=jax.ShapeDtypeStruct(whole, rows.dt...  92.9 us
    psum x1, waiting for transfers between devices, scan_state(): lax.psum(jnp.dot(x_in, xproj_w, preferred_element_type=jnp.float32), 'ten...  68.4 us
    unnamed x44, local copies, waits for them, and re-layouts  4.55 us
    reshape x1, local copies, waits for them, and re-layouts, per_device(): rest[:, :, 128:128 + side_size // state_size].reshape(slots, side_size)  4.26 us
  transfers between devices with their start and end apart: 1, of which 1 were waited for; matrix products, arithmetic and copies ran while one was open for 2% of the time, Pallas kernels for 0%

profile of v2, /device:TPU:6, one launch (start us, length us, event | category | flops | bytes accessed | tf_op | source)
XLA Modules:
  0.0 211.2 jit_solution(3746409676399628384)
XLA Ops:
  7.2 0.0 copy-start
  7.2 0.0 copy-start.1
  7.2 0.0 copy-start.18
  7.2 0.0 copy-start.17
  7.2 0.0 copy-start.13
  7.2 0.0 copy-start.14
  7.3 0.0 all-reduce.5.cloned.1.call-start
  7.3 1.6 slice_reduce_fusion
  8.9 0.1 reshape_squeeze.3
  9.0 0.0 copy-done
  9.0 1.1 fusion.65
  10.1 0.0 all-reduce.5.cloned.1.call-update
  10.2 0.0 copy-done.18
  10.2 0.2 convert_reduce_fusion
  10.4 0.1 select_reduce_fusion.1
  10.5 0.1 fusion.48
  10.6 0.1 iota_compare_fusion.5
  10.7 0.0 copy-done.1
  10.7 1.0 fusion.60
  11.7 0.6 exponential_negate_fusion
  12.3 0.1 copy.76
  12.4 0.0 copy-start.3
  12.4 0.0 copy-start.15
  12.4 0.1 reshape.442
  12.5 0.1 broadcast_compare_fusion
  12.6 0.0 copy-done.7
  12.6 0.2 fusion.6
  12.8 0.2 fusion.64
  13.0 0.4 convolution_convert_fusion
  13.4 0.1 iota_compare_fusion.3
  13.4 0.2 select_select_fusion
  13.7 0.0 copy-start.4
  13.7 0.7 copy.130
  14.4 0.7 copy.95
  15.1 68.4 %all-reduce.5.cloned.1.call-done = f32[48,544]{1,0:T(8,128)} async-done(((f32[48,544]{1,0:T(8,128)}), f32[48,544]{1,0:T(8,128)}) %all-reduce.5.cloned.1.call-update) | async-done | bytes 104464 | tf_op jit(solution)/shard_map/psum | solution.py:70
  83.4 0.9 fusion.61
  84.3 0.6 fusion.63
  84.9 0.6 fusion.62
  85.6 1.2 compare_select_fusion
  86.8 0.1 reshape.438
  86.9 0.1 fusion.59
  87.1 0.0 copy-start.9
  87.1 0.0 copy-start.16
  87.1 1.0 copy_bitcast_fusion.2
  88.1 0.0 copy-start.5
  88.1 0.0 copy-start.8
  88.2 2.3 %multiply_reduce_fusion.1 = (f32[16,1024]{1,0:T(8,128)S(1)}, f32[16,1024]{1,0:T(8,128)S(1)}, f32[16,1024]{1,0:T(8,128)S(1)}, bf16[16,16,1024]{2,1,0:T(8,128)(2,1)S(1)}) fusion(f32[16,16]{1,0:T(8,128)} %bitcast.120, f32[16,1024]{1,0:T(8,128)S(1)} %get-tuple-element.63, f32[16,16]{1,0:T(8,128)} %bitcast.116, f32[16,1024]{1,0:T(8,128)S(1)} %get-tuple-element.44, ...), kind=kLoop, calls=%fused_computation.13 | loop fusion | flops 4931584 | bytes 2234368 | tf_op jit(solution)/shard_map/reduce_sum | solution.py:88
  90.5 0.1 fusion.26
  90.7 0.7 reshape.444
  91.5 0.1 fusion.12
  91.6 0.1 fusion.7.rows
  91.7 92.9 %move_rows.1 = bf16[2,8,8,16,896]{4,3,2,1,0:T(8,128)(2,1)S(1)} custom-call(s32[64]{0:T(128)S(1)} %broadcast_select_fusion.chosen, bf16[2,17,16,896]{3,2,1,0:T(8,128)(2,1)S(1)} %fusion.7.rows), custom_call_target="tpu_custom_call" | custom-call | tf_op jit(solution)/shard_map/move_rows/pallas_call | solution.py:167
  184.5 0.4 fusion.57
  184.9 0.8 slice.146
  185.7 1.3 slice.143
  186.9 4.3 %reshape.445 = bf16[64,11008]{1,0:T(8,128)(2,1)} reshape(bf16[64,16,688]{2,1,0:T(8,128)(2,1)} %slice.143) | data formatting | bytes 2818048 | tf_op jit(solution)/shard_map/reshape | solution.py:226
  191.2 1.9 slice.147
  193.1 1.9 fusion.58
  195.1 0.8 copy.129
  195.8 1.7 reshape.447
  197.5 0.9 copy.79
  198.4 2.2 %reshape.448 = bf16[64,19,1,256]{3,1,0,2:T(8,128)(2,1)} reshape(bf16[64,4864]{1,0:T(8,128)(2,1)} %slice.147) | data formatting | bytes 1245184 | tf_op jit(solution)/shard_map/reshape | solution.py:232
  200.6 2.1 copy.80
  202.7 1.6 pad_maximum_fusion
  (37 shorter events, 0.3 us)
Async XLA Ops:
  7.2 1.8 copy-start
  7.2 3.5 %copy-start.1 = (bf16[16,3,2,1024]{3,2,1,0:T(2,128)(2,1)S(1)}, bf16[16,3,2,1024]{3,2,1,0:T(2,128)(2,1)}, u32[]{:S(2)}) copy-start(bf16[16,3,2,1024]{3,2,1,0:T(2,128)(2,1)} %param.12) | copy-start | bytes 589828
  7.2 3.0 %copy-start.18 = (s32[16,1]{0,1:T(1,128)S(1)}, s32[16,1]{0,1:T(1,128)}, u32[]{:S(2)}) copy-start(s32[16,1]{0,1:T(1,128)} %param.18) | copy-start | bytes 196
  7.2 3.4 %copy-start.17 = (s32[16]{0:T(128)S(1)}, s32[16]{0:T(128)}, u32[]{:S(2)}) copy-start(s32[16]{0:T(128)} %param.17) | copy-start | bytes 196
  7.2 3.5 %copy-start.13 = (bf16[16,3,1,256]{3,0,2,1:T(8,128)(2,1)S(1)}, bf16[16,3,1,256]{3,0,2,1:T(8,128)(2,1)}, u32[]{:S(2)}) copy-start(bf16[16,3,1,256]{3,0,2,1:T(8,128)(2,1)} %param.14) | copy-start | bytes 73732
  7.2 4.4 %copy-start.14 = (f32[16,1024]{1,0:T(8,128)S(1)}, f32[16,1024]{1,0:T(8,128)}, u32[]{:S(2)}) copy-start(f32[16,1024]{1,0:T(8,128)} %param.22) | copy-start | bytes 196612
  7.2 5.1 %copy-start.12 = (bf16[16,3,1,1024]{3,0,2,1:T(8,128)(2,1)S(1)}, bf16[16,3,1,1024]{3,0,2,1:T(8,128)(2,1)}, u32[]{:S(2)}) copy-start(bf16[16,3,1,1024]{3,0,2,1:T(8,128)(2,1)} %param.13) | copy-start | bytes 294916
  7.2 5.3 %copy-start.7 = (bf16[16,16,1,256]{3,1,2,0:T(8,128)(2,1)S(1)}, bf16[16,16,1,256]{3,1,2,0:T(8,128)(2,1)}, u32[]{:S(2)}) copy-start(bf16[16,16,1,256]{3,1,2,0:T(8,128)(2,1)} %param.16) | copy-start | bytes 393220
  7.3 76.2 %all-reduce.5.cloned.1.call-start = ((), (), s32[]{:S(2)}) async-start(), calls=%async_computation | async-start | bytes 245760 | tf_op jit(solution)/shard_map/psum | solution.py:70
  12.4 73.2 %copy-start.3 = (bf16[512,1024]{1,0:T(8,128)(2,1)S(1)}, bf16[512,1024]{1,0:T(8,128)(2,1)}, u32[]{:S(2)}) copy-start(bf16[512,1024]{1,0:T(8,128)(2,1)} %param.20) | copy-start | bytes 3145732
  12.4 73.2 %copy-start.15 = (f32[1024]{0:T(1024)S(1)}, f32[1024]{0:T(1024)}, u32[]{:S(2)}) copy-start(f32[1024]{0:T(1024)} %param.21) | copy-start | bytes 12292
  13.7 74.4 %copy-start.4 = (f32[16,16,1024]{2,1,0:T(8,128)S(1)}, f32[16,16,1024]{2,1,0:T(8,128)}, u32[]{:S(2)}) copy-start(f32[16,16,1024]{2,1,0:T(8,128)} %param.15) | copy-start | bytes 3145732
  87.1 3.4 %copy-start.6 = (bf16[16,1,1,1024]{3,2,1,0:T(2,128)(2,1)S(1)}, bf16[16,1,1,1024]{3,2,1,0:T(2,128)(2,1)}, u32[]{:S(2)}) copy-start(bf16[16,1,1,1024]{3,2,1,0:T(2,128)(2,1)} %get-tuple-element.35) | copy-start | bytes 98308
  87.1 3.4 %copy-start.9 = (bf16[16,1,1,1024]{3,2,1,0:T(2,128)(2,1)S(1)}, bf16[16,1,1,1024]{3,2,1,0:T(2,128)(2,1)}, u32[]{:S(2)}) copy-start(bf16[16,1,1,1024]{3,2,1,0:T(2,128)(2,1)} %get-tuple-element.31) | copy-start | bytes 98308
  87.1 3.4 %copy-start.10 = (bf16[16,1,1,1024]{3,2,1,0:T(2,128)(2,1)S(1)}, bf16[16,1,1,1024]{3,2,1,0:T(2,128)(2,1)}, u32[]{:S(2)}) copy-start(bf16[16,1,1,1024]{3,2,1,0:T(2,128)(2,1)} %get-tuple-element.32) | copy-start | bytes 98308
  87.1 3.4 %copy-start.11 = (bf16[16,1,1,1024]{3,2,1,0:T(2,128)(2,1)S(1)}, bf16[16,1,1,1024]{3,2,1,0:T(2,128)(2,1)}, u32[]{:S(2)}) copy-start(bf16[16,1,1,1024]{3,2,1,0:T(2,128)(2,1)} %get-tuple-element.36) | copy-start | bytes 98308
  87.1 3.4 %copy-start.16 = (f32[1024]{0:T(1024)S(1)}, f32[1024]{0:T(1024)}, u32[]{:S(2)}) copy-start(f32[1024]{0:T(1024)} %param.23) | copy-start | bytes 12292
  88.1 2.6 %copy-start.5 = (bf16[2,8,19,256]{3,1,2,0:T(8,128)(2,1)S(1)}, bf16[2,8,19,256]{3,1,2,0:T(8,128)(2,1)}, u32[]{:S(2)}) copy-start(bf16[2,8,19,256]{3,1,2,0:T(8,128)(2,1)} %copy.95) | copy-start | bytes 466948
  88.1 2.6 %copy-start.8 = (bf16[2,8,24,128]{3,1,2,0:T(8,128)(2,1)S(1)}, bf16[2,8,24,128]{3,1,2,0:T(8,128)(2,1)}, u32[]{:S(2)}) copy-start(bf16[2,8,24,128]{3,1,2,0:T(8,128)(2,1)} %copy.130) | copy-start | bytes 294916
  198.4 4.3 %copy-start.2 = (bf16[64,16,128]{2,1,0:T(8,128)(2,1)S(1)}, bf16[64,16,128]{2,1,0:T(8,128)(2,1)}, u32[]{:S(2)}) copy-start(bf16[64,16,128]{2,1,0:T(8,128)(2,1)} %slice.146) | copy-start | bytes 786436
Sparse Core Ops, SparseCore 0:
  11.0 72.3 all-reduce.4

commit v3 on v2

--- a/solution.py
+++ b/solution.py
@@ -8,18 +8,6 @@
 MESH = pl.DeviceIdType.MESH
 SIDE = 8
 NEAR_FIRST = (1, 7, 2, 6, 3, 5, 4)
-
-
-def extend_pages(kv_pages, new_kv, lengths):
-    row_count = kv_pages.shape[0]
-    step_count = new_kv.shape[1]
-    padding = jnp.zeros((row_count, step_count) + kv_pages.shape[2:], kv_pages.dtype)
-    grown = jnp.concatenate([kv_pages, padding], axis=1)
-    position = jnp.arange(grown.shape[1], dtype=jnp.int32)[None, :]
-    for offset in range(step_count):
-        hit = (position == lengths[:, None] + offset)[:, :, None, None]
-        grown = jnp.where(hit, new_kv[:, offset][:, None], grown)
-    return grown
 
 
 def sending_rows(destination, peer_count):
@@ -36,58 +24,335 @@
     return jnp.sum(jnp.where(matches, row_ids[None, :], 0), axis=1), jnp.any(matches, axis=1)
 
 
-def attend(queries, new_kv, kv_cache, lengths):
-    rows, steps, _, query_width = queries.shape
-    context = kv_cache.shape[1]
-    width = kv_cache.shape[3] // 2
+def swap_matrix(first, second):
+    size = first * second
+    row = lax.broadcasted_iota(jnp.int32, (size, size), 0)
+    column = lax.broadcasted_iota(jnp.int32, (size, size), 1)
+    return ((row % second) * first + row // second == column).astype(jnp.bfloat16)
+
+
+def swap_rows(blocks):
+    first, second, width = blocks.shape
+    swapped = jnp.dot(
+        swap_matrix(second, first),
+        blocks.reshape(first * second, width),
+        preferred_element_type=jnp.float32,
+    )
+    return swapped.astype(jnp.bfloat16).reshape(second, first, width)
+
+
+def project_kernel(mamba, weights, total, part, arrived, sum_sent, sum_come, sent, come):
+    me = lax.axis_index("tensor")
+    peers = lax.axis_size("tensor")
+    here = lax.axis_index("replica")
+    barrier = pltpu.get_barrier_semaphore()
+    for hop in range(1, peers):
+        peer = (here, lax.rem(me + hop, peers))
+        pl.semaphore_signal(barrier, inc=1, device_id=peer, device_id_type=MESH)
+    steps, _, rows, width = mamba.shape
+    chunk = part.shape[1]
+    per_step = rows // chunk
+    for step in range(steps):
+        block = lax.dot_general(
+            mamba[step, 0],
+            weights[...],
+            (((1,), (1,)), ((), ())),
+            preferred_element_type=jnp.float32,
+        )
+        for piece in range(per_step):
+            part[step * per_step + piece] = block[piece * chunk : (piece + 1) * chunk]
+    for piece in range(steps * per_step, peers):
+        part[piece] = jnp.zeros(part.shape[1:], part.dtype)
+    pl.semaphore_wait(barrier, peers - 1)
+
+    copies = []
+    for hop in range(1, peers):
+        target = lax.rem(me + hop, peers)
+        copy = pltpu.make_async_remote_copy(
+            src_ref=part.at[target],
+            dst_ref=arrived.at[hop],
+            send_sem=sum_sent.at[hop],
+            recv_sem=sum_come.at[hop],
+            device_id=(here, target),
+            device_id_type=MESH,
+        )
+        copy.start()
+        copies.append(copy)
+    summed = part[me]
+    for hop in range(1, peers):
+        copies[hop - 1].wait_recv()
+        summed = summed + arrived[hop]
+    total[me] = summed
+    for hop in range(1, peers):
+        target = lax.rem(me + hop, peers)
+        copy = pltpu.make_async_remote_copy(
+            src_ref=total.at[me],
+            dst_ref=total.at[me],
+            send_sem=sent.at[hop],
+            recv_sem=come.at[hop],
+            device_id=(here, target),
+            device_id_type=MESH,
+        )
+        copy.start()
+        copies.append(copy)
+    for copy in copies[: peers - 1]:
+        copy.wait_send()
+    for copy in copies[peers - 1 :]:
+        copy.wait()
+
+
+def project(mamba, weights):
+    chunk = 8
+    peers = lax.axis_size("tensor")
+    shape = (peers, chunk, weights.shape[0])
+    total = pl.pallas_call(
+        project_kernel,
+        out_shape=jax.ShapeDtypeStruct(shape, jnp.float32),
+        in_specs=[pl.BlockSpec(memory_space=pltpu.VMEM)] * 2,
+        out_specs=pl.BlockSpec(memory_space=pltpu.VMEM),
+        scratch_shapes=[
+            pltpu.VMEM(shape, jnp.float32),
+            pltpu.VMEM(shape, jnp.float32),
+        ]
+        + [pltpu.SemaphoreType.DMA((peers,))] * 4,
+        name="project",
+        compiler_params=pltpu.CompilerParams(
+            collective_id=2, has_side_effects=True, vmem_limit_bytes=32 << 20
+        ),
+    )(mamba, weights)
+    return total.reshape(peers * chunk, weights.shape[0])
+
+
+def attend(queries, cached, fresh, lengths):
+    steps, rows, query_width = queries.shape
+    context = cached.shape[1]
+    width = cached.shape[2] // 2
     group = query_width // width
-    query = queries.reshape(rows, steps * group, width)
-    pages = jnp.concatenate([kv_cache[:, :, 0], new_kv[:, :, 0]], axis=1)
-    scores = jnp.einsum(
-        "nqd,nkd->nqk", query, pages[..., :width], preferred_element_type=jnp.float32
+    pages = jnp.concatenate(
+        [cached.reshape(rows * context, 2 * width), fresh.reshape(steps * rows, 2 * width)], axis=0
+    )
+    query = jnp.concatenate(
+        [queries[s, :, g * width : (g + 1) * width] for s in range(steps) for g in range(group)],
+        axis=0,
+    )
+    scores = lax.dot_general(
+        query, pages[:, :width], (((1,), (1,)), ((), ())), preferred_element_type=jnp.float32
     ) * (width ** (-0.5))
-    key_id = jnp.arange(context + steps, dtype=jnp.int32)
-    step_id = jnp.arange(steps * group, dtype=jnp.int32) // group
-    live = jnp.where(
-        (key_id < context)[None, None, :],
-        key_id[None, None, :] < lengths[:, None, None],
-        (key_id[None, :] - context <= step_id[:, None])[None],
-    )
+    asking = lax.broadcasted_iota(jnp.int32, scores.shape, 0)
+    asked = lax.broadcasted_iota(jnp.int32, scores.shape, 1)
+    own, step = asking % rows, asking // (group * rows)
+    new = asked - rows * context
+    cache_live = (new < 0) & (asked // context == own) & (asked % context < lengths)
+    fresh_live = (new >= 0) & (new % rows == own) & (new // rows <= step)
+    live = cache_live | fresh_live
     top = jnp.max(jnp.where(live, scores, -1e30), axis=-1, keepdims=True)
     raised = jnp.where(live, jnp.exp(scores - top), 0.0)
     weights = (raised / jnp.sum(raised, axis=-1, keepdims=True)).astype(jnp.bfloat16)
-    summed = jnp.einsum(
-        "nqk,nkd->nqd", weights, pages[..., width:], preferred_element_type=jnp.float32
-    )
-    return summed.astype(jnp.bfloat16).reshape(rows, steps, query_width)
-
-
-def scan_state(mamba_in, ssm_state, xproj_w, dtproj_w, dt_bias, a_log, d_skip):
-    rows, steps, _, width = mamba_in.shape
+    summed = jnp.dot(weights, pages[:, width:], preferred_element_type=jnp.float32)
+    summed = summed.astype(jnp.bfloat16)
+    return [
+        [summed[(s * group + g) * rows : (s * group + g + 1) * rows] for g in range(group)]
+        for s in range(steps)
+    ]
+
+
+def grow(cached, fresh, lengths):
+    rows, context, width = cached.shape
+    steps = fresh.shape[0]
+    shape = (rows * context, steps * rows)
+    place = lax.broadcasted_iota(jnp.int32, shape, 0)
+    token = lax.broadcasted_iota(jnp.int32, shape, 1)
+    hit = (place // context == token % rows) & (place % context == lengths + token // rows)
+    chosen = jnp.dot(
+        hit.astype(jnp.bfloat16),
+        fresh.reshape(steps * rows, width),
+        preferred_element_type=jnp.float32,
+    )
+    written = jnp.max(hit.astype(jnp.float32), axis=1, keepdims=True) > 0.0
+    kept = cached.reshape(rows * context, width).astype(jnp.float32)
+    shape = (steps * rows, steps * rows)
+    place = lax.broadcasted_iota(jnp.int32, shape, 0)
+    token = lax.broadcasted_iota(jnp.int32, shape, 1)
+    hit = (place % rows == token % rows) & (context + place // rows == lengths + token // rows)
+    tail = jnp.dot(
+        hit.astype(jnp.bfloat16),
+        fresh.reshape(steps * rows, width),
+        preferred_element_type=jnp.float32,
+    )
+    grown = jnp.where(written, chosen, kept).astype(jnp.bfloat16)
+    return grown.reshape(rows, context, width), tail.astype(jnp.bfloat16).reshape(steps, rows, width)
+
+
+def decode_kernel(
+    mamba,
+    queries,
+    fresh,
+    state,
+    cached,
+    key_lengths,
+    token_lengths,
+    total,
+    dtproj_w,
+    dt_bias,
+    a_log,
+    d_skip,
+    packed,
+    decay_rate,
+    step_size,
+    b_wide,
+    c_wide,
+    readout,
+):
+    steps, _, rows, width = mamba.shape
     low_width = dtproj_w.shape[0]
     state_size = a_log.shape[0]
-    x_in = mamba_in[:, :, 0].reshape(rows * steps, width)
-    projected = lax.psum(jnp.dot(x_in, xproj_w, preferred_element_type=jnp.float32), "tensor")
-    low_rank = projected[:, :low_width].astype(jnp.bfloat16)
-    step_size = jax.nn.softplus(
-        jnp.dot(low_rank, dtproj_w, preferred_element_type=jnp.float32) + dt_bias
-    ).reshape(rows, steps, width)
-    b_all = projected[:, low_width : low_width + state_size].reshape(rows, steps, state_size)
-    c_all = projected[:, low_width + state_size :].reshape(rows, steps, state_size)
-    decay_rate = -jnp.exp(a_log)
-    carry = ssm_state
-    mixed = []
+    lane = 128
+    page_width = cached.shape[2]
+    cut = packed.shape[3] - page_width
+    rest = width - cut
+
+    grown, tail = grow(cached[...], fresh[...], token_lengths[...])
+    packed[0, :rows, :, cut:] = grown
+    attended = attend(queries[...], cached[...], fresh[...], key_lengths[...])
+    per_block = page_width // lane
+    blocks = [tail[s] for s in range(steps)]
     for step in range(steps):
-        x_float = mamba_in[:, step, 0].astype(jnp.float32)
-        z_float = mamba_in[:, step, 1].astype(jnp.float32)
-        size = step_size[:, step]
-        carry = (
-            jnp.exp(size[:, None, :] * decay_rate[None]) * carry
-            + b_all[:, step, :, None] * (size * x_float)[:, None, :]
-        )
-        readout = jnp.sum(carry * c_all[:, step, :, None], axis=1) + d_skip * x_float
-        mixed.append((readout * jax.nn.silu(z_float)).astype(jnp.bfloat16))
-    return jnp.stack(mixed, axis=1), carry.astype(jnp.bfloat16)
+        for g in range(0, len(attended[step]), per_block):
+            blocks.append(jnp.concatenate(attended[step][g : g + per_block], axis=1))
+    while len(blocks) < state_size:
+        blocks.append(jnp.zeros((rows, page_width), jnp.bfloat16))
+    packed[1, :rows, :, cut:] = swap_rows(jnp.stack(blocks))
+    packed[0, rows] = jnp.zeros(packed.shape[2:], packed.dtype)
+    packed[1, rows] = jnp.zeros(packed.shape[2:], packed.dtype)
+
+    low_rank = total[: steps * rows, :low_width].astype(jnp.bfloat16)
+    raw = jnp.dot(low_rank, dtproj_w[...], preferred_element_type=jnp.float32) + dt_bias[...]
+    step_size[...] = jnp.maximum(raw, 0.0) + jnp.log1p(jnp.exp(-jnp.abs(raw)))
+    decay_rate[...] = -jnp.exp(a_log[...])
+    turned = jnp.transpose(total[: steps * rows, low_width:])
+    for index in range(steps * rows):
+        column = turned[:, index : index + 1]
+        b_wide[index] = jnp.broadcast_to(column[:state_size], (state_size, lane))
+        c_wide[index] = jnp.broadcast_to(column[state_size:], (state_size, lane))
+
+    for row in range(rows):
+        for start in range(0, width, lane):
+            span = slice(start, start + lane)
+            carry = state[row, :, span]
+            for step in range(steps):
+                index = step * rows + row
+                size = step_size[index : index + 1, span]
+                x = mamba[step, 0, row : row + 1, span].astype(jnp.float32)
+                carry = jnp.exp(size * decay_rate[:, span]) * carry + b_wide[index] * (size * x)
+                readout[index : index + 1, span] = jnp.sum(
+                    c_wide[index] * carry, axis=0, keepdims=True
+                )
+            rounded = carry.astype(jnp.bfloat16)
+            if start < cut:
+                packed[0, row, :, span] = rounded
+            else:
+                packed[1, row, :, start - cut : start - cut + lane] = rounded
+
+    blocks = []
+    for step in range(steps):
+        x = mamba[step, 0].astype(jnp.float32)
+        z = mamba[step, 1].astype(jnp.float32)
+        whole = readout[step * rows : (step + 1) * rows] + d_skip[...] * x
+        mixed = (whole * (z / (1.0 + jnp.exp(-z)))).astype(jnp.bfloat16)
+        for start in range(0, width, page_width):
+            blocks.append(mixed[:, start : start + page_width])
+    while len(blocks) < state_size:
+        blocks.append(jnp.zeros((rows, page_width), jnp.bfloat16))
+    packed[1, :rows, :, rest:cut] = swap_rows(jnp.stack(blocks))
+
+
+def decode(mamba, queries, fresh, state, cached, lengths, total, dtproj_w, dt_bias, a_log, d_skip):
+    steps, _, rows, width = mamba.shape
+    context = cached.shape[1]
+    page_width = cached.shape[2]
+    state_size = a_log.shape[0]
+    key_lengths = jnp.concatenate([jnp.repeat(lengths, context), jnp.tile(lengths, steps)])
+    token_lengths = jnp.tile(lengths, steps)
+    half = (width + 3 * page_width) // 2
+    operands = (
+        mamba,
+        queries,
+        fresh,
+        state,
+        cached,
+        key_lengths[None],
+        token_lengths[None],
+        total,
+        dtproj_w,
+        dt_bias[None],
+        a_log,
+        d_skip[None],
+    )
+    return pl.pallas_call(
+        decode_kernel,
+        out_shape=jax.ShapeDtypeStruct((2, rows + 1, state_size, half), jnp.bfloat16),
+        in_specs=[pl.BlockSpec(memory_space=pltpu.VMEM)] * len(operands),
+        out_specs=pl.BlockSpec(memory_space=pltpu.VMEM),
+        scratch_shapes=[
+            pltpu.VMEM((state_size, width), jnp.float32),
+            pltpu.VMEM((steps * rows, width), jnp.float32),
+            pltpu.VMEM((steps * rows, state_size, 128), jnp.float32),
+            pltpu.VMEM((steps * rows, state_size, 128), jnp.float32),
+            pltpu.VMEM((steps * rows, width), jnp.float32),
+        ],
+        name="decode",
+        compiler_params=pltpu.CompilerParams(vmem_limit_bytes=32 << 20),
+    )(*operands)
+
+
+def unpack_kernel(main, rest, mixed, attended, state, pages):
+    steps, _, width = mixed.shape
+    page_width = pages.shape[2]
+    cut = main.shape[3] - page_width
+    left = width - cut
+    context = main.shape[2]
+    state[:, :, :cut] = main[0, :, :, :cut]
+    state[:, :, cut:] = rest[0, :, :, :left]
+    pages[:context] = swap_rows(main[0, :, :, cut:])
+    swapped = swap_rows(rest[0, :, :, cut:])
+    pages[context:] = swapped[:steps]
+    per_step = width // page_width
+    for step in range(steps):
+        for piece in range(per_step):
+            span = slice(piece * page_width, (piece + 1) * page_width)
+            attended[step, :, span] = swapped[steps + step * per_step + piece]
+    swapped = swap_rows(rest[0, :, :, left:cut])
+    for step in range(steps):
+        for piece in range(per_step):
+            span = slice(piece * page_width, (piece + 1) * page_width)
+            mixed[step, :, span] = swapped[step * per_step + piece]
+
+
+def unpack(moved, steps, width, page_width):
+    _, slots, state_size, half = moved.shape
+    block = 16
+    return pl.pallas_call(
+        unpack_kernel,
+        grid=(slots // block,),
+        out_shape=(
+            jax.ShapeDtypeStruct((steps, slots, width), jnp.bfloat16),
+            jax.ShapeDtypeStruct((steps, slots, width), jnp.bfloat16),
+            jax.ShapeDtypeStruct((slots, state_size, width), jnp.bfloat16),
+            jax.ShapeDtypeStruct((state_size + steps, slots, page_width), jnp.bfloat16),
+        ),
+        in_specs=[
+            pl.BlockSpec((1, block, state_size, half), lambda i: (0, i, 0, 0)),
+            pl.BlockSpec((1, block, state_size, half), lambda i: (1, i, 0, 0)),
+        ],
+        out_specs=(
+            pl.BlockSpec((steps, block, width), lambda i: (0, i, 0)),
+            pl.BlockSpec((steps, block, width), lambda i: (0, i, 0)),
+            pl.BlockSpec((block, state_size, width), lambda i: (i, 0, 0)),
+            pl.BlockSpec((state_size + steps, block, page_width), lambda i: (0, i, 0)),
+        ),
+        name="unpack",
+        compiler_params=pltpu.CompilerParams(vmem_limit_bytes=32 << 20),
+    )(moved, moved)
 
 
 def move_kernel(chosen, rows, out, placed, middle, first_sent, first_come, sent, come):
@@ -204,32 +469,29 @@
 ):
     chosen, present = sending_rows(destination, lax.axis_size("replica"))
     rows, steps, _, width = mamba_in.shape
-    state_size = a_log.shape[0]
-    query_width = queries.shape[3]
     chosen = jnp.where(present, chosen, rows)
-    attended = attend(queries, new_kv, kv_cache, lengths)
-    grown = extend_pages(kv_cache, new_kv, lengths)
-    mixed, state = scan_state(mamba_in, ssm_state, xproj_w, dtproj_w, dt_bias, a_log, d_skip)
-    side = jnp.concatenate(
-        [mixed.reshape(rows, -1), attended.reshape(rows, -1), grown.reshape(rows, -1)], axis=1
-    )
-    side_size = side.shape[1]
-    side = side.reshape(rows, state_size, -1)
-    cut = width - 128
-    half = jnp.concatenate([state[:, :, cut:], side], axis=2)
-    half = jnp.pad(half, ((0, 0), (0, 0), (0, cut - half.shape[2])))
-    both = jnp.stack([state[:, :, :cut], half])
-    both = jnp.pad(both, ((0, 0), (0, 1), (0, 0), (0, 0)))
-    main, rest = move_rows(both, chosen)
-    slots = main.shape[0]
-    out_state = jnp.concatenate([main, rest[:, :, :128]], axis=2)
-    rest = rest[:, :, 128 : 128 + side_size // state_size].reshape(slots, side_size)
-    mixed_size, attended_size = steps * width, steps * query_width
+    mamba = jnp.transpose(mamba_in, (1, 2, 0, 3))
+    total = project(mamba, xproj_w.T)
+    packed = decode(
+        mamba,
+        jnp.transpose(queries[:, :, 0], (1, 0, 2)),
+        jnp.transpose(new_kv[:, :, 0], (1, 0, 2)),
+        ssm_state,
+        kv_cache[:, :, 0],
+        lengths,
+        total,
+        dtproj_w,
+        dt_bias,
+        a_log,
+        d_skip,
+    )
+    moved = move_rows(packed, chosen)
+    mixed, attended, state, pages = unpack(moved, steps, width, kv_cache.shape[3])
     return (
-        rest[:, :mixed_size].reshape(slots, steps, width),
-        rest[:, mixed_size : mixed_size + attended_size].reshape(slots, steps, 1, query_width),
-        out_state,
-        rest[:, mixed_size + attended_size :].reshape((slots,) + grown.shape[1:]),
+        jnp.transpose(mixed, (1, 0, 2)),
+        jnp.transpose(attended, (1, 0, 2))[:, :, None],
+        state,
+        jnp.transpose(pages, (1, 0, 2))[:, :, None],
     )
 
 

time: 212 us -> 126 us (0.59)
  waiting for transfers between devices: 68.4 us -> 0 us
  Pallas kernels: 92.9 us -> 112 us
  local copies, waits for them, and re-layouts: 25.6 us -> 9.81 us
  between operations: 14.5 us -> 0.7 us
  other arithmetic: 6.85 us -> 1.77 us
  matrix products: 2.93 us -> 0 us
    psum x1 -> x0, waiting for transfers between devices: 68.4 us -> none  [scan_state(): lax.psum(jnp.dot(x_in, xproj_w, preferred_element_type=jnp.float32), 'ten...]
    pallas_call x0 -> x3, Pallas kernels: none -> 20.5 us  [the longest x1 15.1 us: project(): pl.pallas_call(project_kernel, out_shape=jax.ShapeDtypeStruct(shape, jnp....]
    slice x11 -> x0, local copies, waits for them, and re-layouts: 10.7 us -> none  [the longest x1 1.94 us: per_device(): rest[:, mixed_size + attended_size:].reshape((slots,) + grown.shape[1:])]
    reshape x10 -> x1, local copies, waits for them, and re-layouts: 9.86 us -> 0.08 us  [decode(): jnp.repeat(lengths, context)]
    unnamed x44 -> x19, local copies, waits for them, and re-layouts: 4.55 us -> 8.18 us
    dot_general x4 -> x0, matrix products: 2.93 us -> none  [the longest x1 1.24 us: scan_state(): jnp.dot(low_rank, dtproj_w, preferred_element_type=jnp.float32) + dt_bias]
    reduce_sum x1 -> x0, other arithmetic: 2.25 us -> none  [scan_state(): jnp.sum(carry * c_all[:, step, :, None], axis=1) + d_skip * x_float]
  transfers between devices with their start and end apart: 1 -> 0, of which waited for: 1 -> 0; matrix products, arithmetic and copies ran while one was open for 2% -> 0% of each run, Pallas kernels for 0% -> 0%
where the time goes in v3:
time: 126 us; the launch traced here: 124 us
  Pallas kernels  112 us (89%)
  local copies, waits for them, and re-layouts  9.81 us (8%)
  other arithmetic  1.77 us (1%)
    pallas_call x1, Pallas kernels, move_rows(): pl.pallas_call(move_kernel, out_shape=jax.ShapeDtypeStruct(whole, rows.dt...  91.4 us
    pallas_call x1, Pallas kernels, project(): pl.pallas_call(project_kernel, out_shape=jax.ShapeDtypeStruct(shape, jnp....  15.1 us
    unnamed x19, local copies, waits for them, and re-layouts  8.18 us
    pallas_call x1, Pallas kernels, unpack(): pl.pallas_call(unpack_kernel, grid=(slots // block,), out_shape=(jax.Shap...  2.84 us
    pallas_call x1, Pallas kernels, decode(): pl.pallas_call(decode_kernel, out_shape=jax.ShapeDtypeStruct((2, rows + 1...  2.57 us

profile of v3, /device:TPU:6, one launch (start us, length us, event | category | flops | bytes accessed | tf_op | source)
XLA Modules:
  0.0 124.2 jit_solution(441177921525530389)
XLA Ops:
  0.6 0.9 convert_reduce_fusion
  1.5 0.7 bitcast_add_fusion
  2.2 0.1 select_reduce_fusion
  2.3 0.1 fusion
  2.4 0.7 tile.4
  3.0 0.1 broadcast_in_dim_tile.3.token_lengths
  3.1 0.1 tile.5
  3.2 0.7 broadcast_in_dim.42
  3.9 0.1 reshape.26
  4.0 1.0 copy.23
  5.0 0.0 copy-start
  5.0 1.2 copy-done
  6.3 0.0 copy-start.1
  6.3 15.1 %project.1 = f32[8,8,544]{2,1,0:T(8,128)S(1)} custom-call(bf16[3,2,16,1024]{3,2,1,0:T(8,128)(2,1)S(1)} %bitcast.30, bf16[544,1024]{1,0:T(8,128)(2,1)S(1)} %bitcast.32), custom_call_target="tpu_custom_call" | custom-call | tf_op jit(solution)/shard_map/project/pallas_call | solution.py:108
  21.4 0.0 copy-done.1
  21.4 0.0 copy-start.2
  21.4 1.2 copy-done.2
  22.6 0.0 copy-start.3
  22.6 0.9 copy-done.3
  23.5 0.0 copy-start.4
  23.5 0.9 copy-done.4
  24.4 0.0 copy-start.5
  24.4 0.8 copy-done.5
  25.3 0.0 copy-start.6
  25.3 0.7 copy-done.6
  26.0 0.0 copy-start.7
  26.0 0.7 copy-done.7
  26.7 0.0 copy-start.8
  26.7 0.7 copy-done.8
  27.4 2.6 %decode.1.rows = bf16[2,17,16,896]{3,2,1,0:T(8,128)(2,1)S(1)} custom-call(bf16[3,2,16,1024]{3,2,1,0:T(8,128)(2,1)S(1)} %bitcast.31, bf16[3,16,1024]{2,1,0:T(8,128)(2,1)S(1)} %bitcast.35, bf16[3,16,256]{2,1,0:T(8,128)(2,1)S(1)} %bitcast.36, f32[16,16,1024]{2,1,0:T(8,128)S(1)} %copy-done.1, bf16[16,16,256]{2,1,0:T(8,128)(2,1)S(1)} %bitcast.34, ...), custom_call_target="tpu_custom_call" | custom-call | tf_op jit(solution)/shard_map/decode/pallas_call | solution.py:291
  29.9 91.4 %move_rows.1 = bf16[2,8,8,16,896]{4,3,2,1,0:T(8,128)(2,1)S(1)} custom-call(s32[64]{0:T(128)S(1)} %broadcast_select_fusion.chosen, bf16[2,17,16,896]{3,2,1,0:T(8,128)(2,1)S(1)} %decode.1.rows), custom_call_target="tpu_custom_call" | custom-call | tf_op jit(solution)/shard_map/move_rows/pallas_call | solution.py:432
  121.3 2.8 %unpack.1 = (bf16[3,64,1024]{2,1,0:T(8,128)(2,1)}, bf16[3,64,1024]{2,1,0:T(8,128)(2,1)}, bf16[64,16,1024]{2,1,0:T(8,128)(2,1)}, bf16[19,64,256]{2,1,0:T(8,128)(2,1)}) custom-call(bf16[2,64,16,896]{3,2,1,0:T(8,128)(2,1)S(1)} %bitcast.28, bf16[2,64,16,896]{3,2,1,0:T(8,128)(2,1)S(1)} %bitcast.29), custom_call_target="tpu_custom_call" | custom-call | tf_op jit(solution)/shard_map/unpack/pallas_call | solution.py:334
  (3 shorter events, 0.0 us)
Async XLA Ops:
  5.0 1.3 %copy-start = (bf16[1024,544]{0,1:T(8,128)(2,1)S(1)}, bf16[1024,544]{0,1:T(8,128)(2,1)}, u32[]{:S(2)}) copy-start(bf16[1024,544]{0,1:T(8,128)(2,1)} %param.19) | copy-start | bytes 3342340
  6.3 15.1 %copy-start.1 = (f32[16,16,1024]{2,1,0:T(8,128)S(1)}, f32[16,16,1024]{2,1,0:T(8,128)}, u32[]{:S(2)}) copy-start(f32[16,16,1024]{2,1,0:T(8,128)} %state.1) | copy-start | bytes 3145732
  21.4 1.2 copy-start.2
  22.6 0.9 copy-start.3
  23.5 0.9 copy-start.4
  24.4 0.8 copy-start.5
  25.3 0.7 copy-start.6
  26.0 0.7 copy-start.7
  26.7 0.7 copy-start.8

commit v4 on v1

v4 whole, which is shorter than its diff:
```python
import jax
import jax.numpy as jnp
from jax import lax
from jax.experimental import pallas as pl
from jax.experimental.pallas import tpu as pltpu
from jax.sharding import PartitionSpec as P

MESH = pl.DeviceIdType.MESH
SIDE = 8
NEAR_FIRST = (1, 7, 2, 6, 3, 5, 4)


def swap_matrix(first, second):
    size = first * second
    row = lax.broadcasted_iota(jnp.int32, (size, size), 0)
    column = lax.broadcasted_iota(jnp.int32, (size, size), 1)
    return ((row % second) * first + row // second == column).astype(jnp.bfloat16)


def swap_rows(blocks):
    first, second, width = blocks.shape
    swapped = jnp.dot(
        swap_matrix(second, first),
        blocks.reshape(first * second, width),
        preferred_element_type=jnp.float32,
    )
    return swapped.astype(jnp.bfloat16).reshape(second, first, width)


def attend(queries, cached, fresh, lengths):
    steps, rows, query_width = queries.shape
    context = cached.shape[1]
    width = cached.shape[2] // 2
    group = query_width // width
    pages = jnp.concatenate(
        [cached.reshape(rows * context, 2 * width), fresh.reshape(steps * rows, 2 * width)], axis=0
    )
    query = jnp.concatenate(
        [queries[s, :, g * width : (g + 1) * width] for s in range(steps) for g in range(group)],
        axis=0,
    )
    scores = lax.dot_general(
        query, pages[:, :width], (((1,), (1,)), ((), ())), preferred_element_type=jnp.float32
    ) * (width ** (-0.5))
    asking = lax.broadcasted_iota(jnp.int32, scores.shape, 0)
    asked = lax.broadcasted_iota(jnp.int32, scores.shape, 1)
    own, step = asking % rows, asking // (group * rows)
    new = asked - rows * context
    cache_live = (new < 0) & (asked // context == own) & (asked % context < lengths)
    fresh_live = (new >= 0) & (new % rows == own) & (new // rows <= step)
    live = cache_live | fresh_live
    top = jnp.max(jnp.where(live, scores, -1e30), axis=-1, keepdims=True)
    raised = jnp.where(live, jnp.exp(scores - top), 0.0)
    weights = (raised / jnp.sum(raised, axis=-1, keepdims=True)).astype(jnp.bfloat16)
    summed = jnp.dot(weights, pages[:, width:], preferred_element_type=jnp.float32)
    summed = summed.astype(jnp.bfloat16)
    return [
        [summed[(s * group + g) * rows : (s * group + g + 1) * rows] for g in range(group)]
        for s in range(steps)
    ]


def grow(cached, fresh, lengths):
    rows, context, width = cached.shape
    steps = fresh.shape[0]
    shape = (rows * context, steps * rows)
    place = lax.broadcasted_iota(jnp.int32, shape, 0)
    token = lax.broadcasted_iota(jnp.int32, shape, 1)
    hit = (place // context == token % rows) & (place % context == lengths + token // rows)
    chosen = jnp.dot(
        hit.astype(jnp.bfloat16),
        fresh.reshape(steps * rows, width),
        preferred_element_type=jnp.float32,
    )
    written = jnp.max(hit.astype(jnp.float32), axis=1, keepdims=True) > 0.0
    kept = cached.reshape(rows * context, width).astype(jnp.float32)
    shape = (steps * rows, steps * rows)
    place = lax.broadcasted_iota(jnp.int32, shape, 0)
    token = lax.broadcasted_iota(jnp.int32, shape, 1)
    hit = (place % rows == token % rows) & (context + place // rows == lengths + token // rows)
    tail = jnp.dot(
        hit.astype(jnp.bfloat16),
        fresh.reshape(steps * rows, width),
        preferred_element_type=jnp.float32,
    )
    grown = jnp.where(written, chosen, kept).astype(jnp.bfloat16)
    return grown.reshape(rows, context, width), tail.astype(jnp.bfloat16).reshape(steps, rows, width)


def attention_kernel(
    lengths, destination, queries_in, fresh_in, cached_in, packed, chosen, queries, fresh, cached, come
):
    copies = [
        pltpu.make_async_copy(source, held, come.at[index])
        for index, (source, held) in enumerate(
            [(queries_in, queries), (fresh_in, fresh), (cached_in, cached)]
        )
    ]
    for copy in copies:
        copy.start()
    rows, context, page_width = cached.shape
    steps = queries.shape[0]
    state_size = packed.shape[2]

    def clear(slot, carry):
        chosen[slot] = rows
        return carry

    def choose(row, carry):
        chosen[destination[row]] = row
        return carry

    lax.fori_loop(0, chosen.shape[0], clear, 0)
    lax.fori_loop(0, rows, choose, 0)

    token = lax.broadcasted_iota(jnp.int32, (1, steps * rows), 1)
    asked = lax.broadcasted_iota(jnp.int32, (1, rows * context + steps * rows), 1)
    key_row = jnp.where(asked < rows * context, asked // context, (asked - rows * context) % rows)
    key_lengths = jnp.zeros_like(asked)
    token_lengths = jnp.zeros_like(token)
    for row in range(rows):
        key_lengths = jnp.where(key_row == row, lengths[row], key_lengths)
        token_lengths = jnp.where(token % rows == row, lengths[row], token_lengths)
    for copy in copies:
        copy.wait()
    grown, tail = grow(cached[...], fresh[...], token_lengths)
    packed[0, :rows] = grown
    attended = attend(queries[...], cached[...], fresh[...], key_lengths)
    per_block = page_width // 128
    blocks = [tail[s] for s in range(steps)]
    for step in range(steps):
        for g in range(0, len(attended[step]), per_block):
            blocks.append(jnp.concatenate(attended[step][g : g + per_block], axis=1))
    while len(blocks) < state_size:
        blocks.append(jnp.zeros((rows, page_width), jnp.bfloat16))
    packed[1, :rows] = swap_rows(jnp.stack(blocks))
    packed[0, rows] = jnp.zeros(packed.shape[2:], packed.dtype)
    packed[1, rows] = jnp.zeros(packed.shape[2:], packed.dtype)


def attention(queries, fresh, cached, lengths, destination, slots, state_size):
    rows, _, page_width = cached.shape
    arrays = (queries, fresh, cached)
    return pl.pallas_call(
        attention_kernel,
        out_shape=(
            jax.ShapeDtypeStruct((2, rows + 1, state_size, page_width), jnp.bfloat16),
            jax.ShapeDtypeStruct((slots,), jnp.int32),
        ),
        in_specs=[pl.BlockSpec(memory_space=pltpu.SMEM)] * 2
        + [pl.BlockSpec(memory_space=pl.ANY)] * 3,
        out_specs=(
            pl.BlockSpec(memory_space=pltpu.VMEM),
            pl.BlockSpec(memory_space=pltpu.SMEM),
        ),
        scratch_shapes=[pltpu.VMEM(array.shape, array.dtype) for array in arrays]
        + [pltpu.SemaphoreType.DMA((3,))],
        name="attention",
        compiler_params=pltpu.CompilerParams(vmem_limit_bytes=32 << 20),
    )(lengths, destination, *arrays)


def move_kernel(
    chosen,
    early,
    mamba_in,
    xproj_in,
    dtproj_in,
    bias_in,
    a_log_in,
    skip_in,
    state_in,
    out_early,
    out_late,
    mamba,
    xproj,
    dtproj,
    bias,
    a_log,
    skip,
    state,
    part,
    arrived,
    total,
    decay_rate,
    step_size,
    drive,
    b_wide,
    c_wide,
    readout,
    moved_state,
    late_mixed,
    placed_early,
    placed_late,
    middle_early,
    middle_late,
    loaded,
    sum_sent,
    sum_come,
    total_sent,
    total_come,
    first_sent,
    first_come,
    sent,
    come,
    kept,
):
    me = lax.axis_index("replica")
    shard = lax.axis_index("tensor")
    shards = lax.axis_size("tensor")
    place = (me // SIDE, me % SIDE)

    def device(route, first, second):
        return (first * SIDE + second if route == 0 else second * SIDE + first, shard)

    barrier = pltpu.get_barrier_semaphore()
    for hop in range(1, shards):
        peer = (me, lax.rem(shard + hop, shards))
        pl.semaphore_signal(barrier, inc=1, device_id=peer, device_id_type=MESH)
    for route in range(2):
        for hop in NEAR_FIRST:
            peer = device(route, lax.rem(place[route] + hop, SIDE), place[1 - route])
            pl.semaphore_signal(barrier, inc=1, device_id=peer, device_id_type=MESH)

    loads = [
        pltpu.make_async_copy(source, held, loaded.at[index])
        for index, (source, held) in enumerate(
            [
                (mamba_in, mamba),
                (xproj_in, xproj),
                (dtproj_in, dtproj),
                (bias_in, bias),
                (a_log_in, a_log),
                (skip_in, skip),
                (state_in, state),
            ]
        )
    ]
    for load in loads:
        load.start()

    def put_early(index, unused):
        first, second = index // SIDE, index % SIDE
        placed_early[0, first, second] = early[0, chosen[first * SIDE + second]]
        placed_early[1, first, second] = early[1, chosen[second * SIDE + first]]
        return unused

    stages = ((placed_early, middle_early, out_early), (placed_late, middle_late, out_late))
    first_copies = {}

    def send_first(stage):
        placed, middle, _ = stages[stage]
        for hop in NEAR_FIRST:
            for route in range(2):
                target = lax.rem(place[route] + hop, SIDE)
                copy = pltpu.make_async_remote_copy(
                    src_ref=placed.at[route, target],
                    dst_ref=middle.at[route, hop],
                    send_sem=first_sent.at[stage, route, hop],
                    recv_sem=first_come.at[stage, route, hop],
                    device_id=device(route, target, place[1 - route]),
                    device_id_type=MESH,
                )
                copy.start()
                first_copies[stage, route, hop] = copy

    def pass_on(stage, route, bundle, origin):
        mine = place[1 - route]
        out = stages[stage][2]
        pair = (origin, mine) if route == 0 else (mine, origin)
        slot = out.at[route, pair[0], pair[1]]
        for hop in NEAR_FIRST:
            target = lax.rem(mine + hop, SIDE)
            pltpu.make_async_remote_copy(
                src_ref=bundle.at[target],
                dst_ref=slot,
                send_sem=sent.at[stage],
                recv_sem=come.at[stage],
                device_id=device(route, place[route], target),
                device_id_type=MESH,
            ).start()
        pltpu.make_async_copy(bundle.at[mine], slot, kept.at[stage]).start()

    def pass_own(stage):
        for route in range(2):
            pass_on(stage, route, stages[stage][0].at[route, place[route]], place[route])

    def pass_arrived(stage):
        for hop in NEAR_FIRST:
            for route in range(2):
                first_copies[stage, route, hop].wait_recv()
                origin = lax.rem(place[route] + SIDE - hop, SIDE)
                pass_on(stage, route, stages[stage][1].at[route, hop], origin)

    lax.fori_loop(0, SIDE * SIDE, put_early, 0)
    loads[0].wait()
    loads[1].wait()
    steps, _, rows, width = mamba.shape
    chunk = part.shape[1]
    per_step = rows // chunk
    for step in range(steps):
        block = lax.dot_general(
            mamba[step, 0],
            xproj[...],
            (((1,), (1,)), ((), ())),
            preferred_element_type=jnp.float32,
        )
        for piece in range(per_step):
            part[step * per_step + piece] = block[piece * chunk : (piece + 1) * chunk]
    for piece in range(steps * per_step, shards):
        part[piece] = jnp.zeros(part.shape[1:], part.dtype)
    pl.semaphore_wait(barrier, shards - 1 + 2 * len(NEAR_FIRST))

    sums = []
    for hop in range(1, shards):
        target = lax.rem(shard + hop, shards)
        copy = pltpu.make_async_remote_copy(
            src_ref=part.at[target],
            dst_ref=arrived.at[hop],
            send_sem=sum_sent.at[hop],
            recv_sem=sum_come.at[hop],
            device_id=(me, target),
            device_id_type=MESH,
        )
        copy.start()
        sums.append(copy)
    send_first(0)
    pass_own(0)
    for load in loads[2:]:
        load.wait()
    decay_rate[...] = -jnp.exp(a_log[...])
    moved_state[rows] = jnp.zeros(moved_state.shape[1:], moved_state.dtype)
    late_mixed[rows] = jnp.zeros(late_mixed.shape[1:], late_mixed.dtype)

    summed = part[shard]
    for hop in range(1, shards):
        sums[hop - 1].wait_recv()
        summed = summed + arrived[hop]
    total[shard] = summed
    totals = []
    for hop in range(1, shards):
        target = lax.rem(shard + hop, shards)
        copy = pltpu.make_async_remote_copy(
            src_ref=total.at[shard],
            dst_ref=total.at[shard],
            send_sem=total_sent.at[hop],
            recv_sem=total_come.at[hop],
            device_id=(me, target),
            device_id_type=MESH,
        )
        copy.start()
        totals.append(copy)
    for copy in totals:
        copy.wait_recv()

    low_width = dtproj.shape[0]
    state_size = a_log.shape[0]
    lane = 128
    projected = total[...].reshape(shards * chunk, total.shape[2])[: steps * rows]
    low_rank = projected[:, :low_width].astype(jnp.bfloat16)
    raw = jnp.dot(low_rank, dtproj[...], preferred_element_type=jnp.float32) + bias[...]
    step_size[...] = jnp.maximum(raw, 0.0) + jnp.log1p(jnp.exp(-jnp.abs(raw)))
    for step in range(steps):
        span = slice(step * rows, (step + 1) * rows)
        drive[span] = step_size[span] * mamba[step, 0].astype(jnp.float32)
    turned = jnp.transpose(projected[:, low_width:])
    for index in range(steps * rows):
        column = turned[:, index : index + 1]
        b_wide[index] = jnp.broadcast_to(column[:state_size], (state_size, lane))
        c_wide[index] = jnp.broadcast_to(column[state_size:], (state_size, lane))

    cut = placed_late.shape[4]
    rest = width - cut

    def update(piece, unused):
        span = pl.ds(pl.multiple_of(piece * lane, lane), lane)
        rate = decay_rate[:, span]
        for row in range(rows):
            carry = state[row, :, span]
            for step in range(steps):
                index = step * rows + row
                size = step_size[index : index + 1, span]
                carry = (
                    jnp.exp(size * rate) * carry
                    + b_wide[index] * drive[index : index + 1, span]
                )
                readout[index : index + 1, span] = jnp.sum(
                    c_wide[index] * carry, axis=0, keepdims=True
                )
            moved_state[row, :, span] = carry.astype(jnp.bfloat16)
        return unused

    lax.fori_loop(0, width // lane, update, 0)
    page_width = cut - rest
    blocks = []
    for step in range(steps):
        x = mamba[step, 0].astype(jnp.float32)
        z = mamba[step, 1].astype(jnp.float32)
        whole = readout[step * rows : (step + 1) * rows] + skip[...] * x
        mixed = (whole * (z / (1.0 + jnp.exp(-z)))).astype(jnp.bfloat16)
        for start in range(0, width, page_width):
            blocks.append(mixed[:, start : start + page_width])
    while len(blocks) < state_size:
        blocks.append(jnp.zeros((rows, page_width), jnp.bfloat16))
    late_mixed[:rows] = swap_rows(jnp.stack(blocks))

    def put_late(index, unused):
        first, second = index // SIDE, index % SIDE
        placed_late[0, first, second] = moved_state[chosen[first * SIDE + second], :, :cut]
        row = chosen[second * SIDE + first]
        placed_late[1, first, second, :, :rest] = moved_state[row, :, cut:]
        placed_late[1, first, second, :, rest:] = late_mixed[row]
        return unused

    lax.fori_loop(0, SIDE * SIDE, put_late, 0)
    send_first(1)
    pass_own(1)
    pass_arrived(0)
    pass_arrived(1)
    for copy in sums + totals + list(first_copies.values()):
        copy.wait_send()
    for stage in range(2):
        out = stages[stage][2]
        others = out.at[:, :, pl.ds(0, SIDE - 1)]
        own = out.at[:, :, 0]
        pltpu.make_async_copy(own, own, kept.at[stage]).wait()
        pltpu.make_async_copy(others, others, sent.at[stage]).wait()
        pltpu.make_async_copy(others, others, come.at[stage]).wait()


def move_rows(chosen, early, mamba, xproj_w, dtproj_w, dt_bias, a_log, d_skip, state):
    steps, _, rows, width = mamba.shape
    state_size = a_log.shape[0]
    page_width = early.shape[3]
    half = (width + page_width) // 2
    shards = lax.axis_size("tensor")
    arrays = (mamba, xproj_w, dtproj_w, dt_bias, a_log, d_skip, state)
    grid = (2, SIDE, SIDE, state_size)
    early_grid, late_grid = grid + (page_width,), grid + (half,)
    sums = (shards, steps * rows // 6, xproj_w.shape[0])
    outs = pl.pallas_call(
        move_kernel,
        out_shape=(
            jax.ShapeDtypeStruct(early_grid, jnp.bfloat16),
            jax.ShapeDtypeStruct(late_grid, jnp.bfloat16),
        ),
        in_specs=[
            pl.BlockSpec(memory_space=pltpu.SMEM),
            pl.BlockSpec(memory_space=pltpu.VMEM),
        ]
        + [pl.BlockSpec(memory_space=pl.ANY)] * len(arrays),
        out_specs=(pl.BlockSpec(memory_space=pl.ANY), pl.BlockSpec(memory_space=pl.ANY)),
        scratch_shapes=[pltpu.VMEM(array.shape, array.dtype) for array in arrays]
        + [pltpu.VMEM(sums, jnp.float32)] * 3
        + [
            pltpu.VMEM((state_size, width), jnp.float32),
            pltpu.VMEM((steps * rows, width), jnp.float32),
            pltpu.VMEM((steps * rows, width), jnp.float32),
            pltpu.VMEM((steps * rows, state_size, 128), jnp.float32),
            pltpu.VMEM((steps * rows, state_size, 128), jnp.float32),
            pltpu.VMEM((steps * rows, width), jnp.float32),
            pltpu.VMEM((rows + 1, state_size, width), jnp.bfloat16),
            pltpu.VMEM((rows + 1, state_size, page_width), jnp.bfloat16),
            pltpu.VMEM(early_grid, jnp.bfloat16),
            pltpu.VMEM(late_grid, jnp.bfloat16),
            pltpu.VMEM(early_grid, jnp.bfloat16),
            pltpu.VMEM(late_grid, jnp.bfloat16),
            pltpu.SemaphoreType.DMA((len(arrays),)),
        ]
        + [pltpu.SemaphoreType.DMA((shards,))] * 4
        + [pltpu.SemaphoreType.DMA((2, 2, SIDE))] * 2
        + [pltpu.SemaphoreType.DMA((2,))] * 3,
        name="move_rows",
        compiler_params=pltpu.CompilerParams(
            collective_id=1, has_side_effects=True, vmem_limit_bytes=32 << 20
        ),
    )(chosen, early, *arrays)
    return [out.reshape((2, SIDE * SIDE) + out.shape[3:]) for out in outs]


def unpack_kernel(early, late, mixed, attended, state, pages):
    steps, _, width = mixed.shape
    page_width = pages.shape[2]
    cut = late.shape[3]
    left = width - cut
    context = early.shape[2]
    state[:, :, :cut] = late[0]
    state[:, :, cut:] = late[1, :, :, :left]
    pages[:context] = swap_rows(early[0])
    swapped = swap_rows(early[1])
    pages[context:] = swapped[:steps]
    per_step = width // page_width
    for step in range(steps):
        for piece in range(per_step):
            span = slice(piece * page_width, (piece + 1) * page_width)
            attended[step, :, span] = swapped[steps + step * per_step + piece]
    swapped = swap_rows(late[1, :, :, left:])
    for step in range(steps):
        for piece in range(per_step):
            span = slice(piece * page_width, (piece + 1) * page_width)
            mixed[step, :, span] = swapped[step * per_step + piece]


def unpack(early, late, steps, width):
    _, slots, state_size, page_width = early.shape
    half = late.shape[3]
    block = 16
    return pl.pallas_call(
        unpack_kernel,
        grid=(slots // block,),
        out_shape=(
            jax.ShapeDtypeStruct((steps, slots, width), jnp.bfloat16),
            jax.ShapeDtypeStruct((steps, slots, width), jnp.bfloat16),
            jax.ShapeDtypeStruct((slots, state_size, width), jnp.bfloat16),
            jax.ShapeDtypeStruct((state_size + steps, slots, page_width), jnp.bfloat16),
        ),
        in_specs=[
            pl.BlockSpec((2, block, state_size, page_width), lambda i: (0, i, 0, 0)),
            pl.BlockSpec((2, block, state_size, half), lambda i: (0, i, 0, 0)),
        ],
        out_specs=(
            pl.BlockSpec((steps, block, width), lambda i: (0, i, 0)),
            pl.BlockSpec((steps, block, width), lambda i: (0, i, 0)),
            pl.BlockSpec((block, state_size, width), lambda i: (i, 0, 0)),
            pl.BlockSpec((state_size + steps, block, page_width), lambda i: (0, i, 0)),
        ),
        name="unpack",
        compiler_params=pltpu.CompilerParams(vmem_limit_bytes=32 << 20),
    )(early, late)


def per_device(
    mamba_in,
    queries,
    new_kv,
    ssm_state,
    kv_cache,
    lengths,
    destination,
    xproj_w,
    dtproj_w,
    dt_bias,
    a_log,
    d_skip,
):
    steps, width = mamba_in.shape[1], mamba_in.shape[3]
    early, chosen = attention(
        jnp.transpose(queries[:, :, 0], (1, 0, 2)),
        jnp.transpose(new_kv[:, :, 0], (1, 0, 2)),
        kv_cache[:, :, 0],
        lengths,
        destination[:, 0],
        lax.axis_size("replica"),
        a_log.shape[0],
    )
    early, late = move_rows(
        chosen,
        early,
        jnp.transpose(mamba_in, (1, 2, 0, 3)),
        xproj_w.T,
        dtproj_w,
        dt_bias[None],
        a_log,
        d_skip[None],
        ssm_state,
    )
    mixed, attended, state, pages = unpack(early, late, steps, width)
    return (
        jnp.transpose(mixed, (1, 0, 2)),
        jnp.transpose(attended, (1, 0, 2))[:, :, None],
        state,
        jnp.transpose(pages, (1, 0, 2))[:, :, None],
    )


def solution(mesh):
    placed = (
        P("replica", None, None, "tensor"),
        P("replica", None, "tensor", None),
        P("replica", None, "tensor", None),
        P("replica", None, "tensor"),
        P("replica", None, "tensor", None),
        P("replica"),
        P("replica", None),
        P("tensor", None),
        P(None, "tensor"),
        P("tensor"),
        P(None, "tensor"),
        P("tensor"),
    )
    return jax.shard_map(
        per_device,
        mesh=mesh,
        in_specs=placed,
        out_specs=(
            P("replica", None, "tensor"),
            P("replica", None, "tensor", None),
            P("replica", None, "tensor"),
            P("replica", None, "tensor", None),
        ),
        check_vma=False,
    )
```

time: 201 us -> 115 us (0.57)
  the two profiles are of different devices: /device:TPU:101 before, /device:TPU:6 now
where the time goes in v4:
time: 115 us; the launch traced here: 113 us
  Pallas kernels  102 us (89%)
  local copies, waits for them, and re-layouts  10.7 us (9%)
    pallas_call x1, Pallas kernels, move_rows(): pl.pallas_call(move_kernel, out_shape=(jax.ShapeDtypeStruct(early_grid, j...  96.3 us
    unnamed x23, local copies, waits for them, and re-layouts  10.7 us
    pallas_call x1, Pallas kernels, unpack(): pl.pallas_call(unpack_kernel, grid=(slots // block,), out_shape=(jax.Shap...  2.94 us
    pallas_call x1, Pallas kernels, attention(): pl.pallas_call(attention_kernel, out_shape=(jax.ShapeDtypeStruct((2, rows...  2.36 us

profile of v4, /device:TPU:6, one launch (start us, length us, event | category | flops | bytes accessed | tf_op | source)
XLA Modules:
  0.0 113.0 jit_solution(4493624471390851697)
XLA Ops:
  0.6 1.0 copy.20
  1.6 0.0 copy-start.3
  1.6 0.9 copy-done.3
  2.5 0.0 copy-start.4
  2.5 0.9 copy-done.4
  3.4 0.0 copy-start.6
  3.4 0.7 copy-done.6
  4.1 0.0 copy-start.9
  4.1 0.7 copy-done.9
  4.8 0.0 copy-start.10
  4.8 0.7 copy-done.10
  5.4 2.4 %attention.1 = (bf16[2,17,16,256]{3,2,1,0:T(8,128)(2,1)S(1)}, s32[64]{0:T(128)S(1)}) custom-call(s32[16]{0:T(128)S(1)} %copy-done.9, s32[16]{0:T(128)S(1)} %bitcast.36, bf16[3,16,1024]{2,1,0:T(8,128)(2,1)S(1)} %bitcast.32, bf16[3,16,256]{2,1,0:T(8,128)(2,1)S(1)} %bitcast.33, bf16[16,16,256]{2,1,0:T(8,128)(2,1)S(1)} %bitcast.31), custom_call_target="tpu_custom_call" | custom-call | tf_op jit(solution)/shard_map/attention/pallas_call | solution.py:144
  7.8 0.0 copy-start
  7.8 1.2 %copy-done = bf16[1024,544]{0,1:T(8,128)(2,1)S(1)} copy-done((bf16[1024,544]{0,1:T(8,128)(2,1)S(1)}, bf16[1024,544]{0,1:T(8,128)(2,1)}, u32[]{:S(2)}) %copy-start) | copy-done | bytes 1114136
  9.1 0.0 copy-start.1
  9.1 1.2 %copy-done.1 = bf16[512,1024]{1,0:T(8,128)(2,1)S(1)} copy-done((bf16[512,1024]{1,0:T(8,128)(2,1)S(1)}, bf16[512,1024]{1,0:T(8,128)(2,1)}, u32[]{:S(2)}) %copy-start.1) | copy-done | bytes 1048600
  10.3 0.0 copy-start.2
  10.3 1.2 %copy-done.2 = f32[16,16,1024]{2,1,0:T(8,128)S(1)} copy-done((f32[16,16,1024]{2,1,0:T(8,128)S(1)}, f32[16,16,1024]{2,1,0:T(8,128)}, u32[]{:S(2)}) %copy-start.2) | copy-done | bytes 1048600
  11.5 0.0 copy-start.5
  11.5 0.8 copy-done.5
  12.4 0.0 copy-start.7
  12.4 0.7 copy-done.7
  13.0 0.0 copy-start.8
  13.0 0.7 copy-done.8
  13.7 96.3 %move_rows.1 = (bf16[2,8,8,16,256]{4,3,2,1,0:T(8,128)(2,1)S(1)}, bf16[2,8,8,16,640]{4,3,2,1,0:T(8,128)(2,1)S(1)}) custom-call(s32[64]{0:T(128)S(1)} %get-tuple-element.12.chosen, bf16[2,17,16,256]{3,2,1,0:T(8,128)(2,1)S(1)} %get-tuple-element.13.early, bf16[3,2,16,1024]{3,2,1,0:T(8,128)(2,1)S(1)} %bitcast.30, bf16[544,1024]{1,0:T(8,128)(2,1)S(1)} %bitcast.28, ...), custom_call_target="tpu_custom_call" | custom-call | tf_op jit(solution)/shard_map/move_rows/pallas_call | solution.py:441
  110.1 2.9 %unpack.1 = (bf16[3,64,1024]{2,1,0:T(8,128)(2,1)}, bf16[3,64,1024]{2,1,0:T(8,128)(2,1)}, bf16[64,16,1024]{2,1,0:T(8,128)(2,1)}, bf16[19,64,256]{2,1,0:T(8,128)(2,1)}) custom-call(bf16[2,64,16,256]{3,2,1,0:T(8,128)(2,1)S(1)} %bitcast.29, bf16[2,64,16,640]{3,2,1,0:T(8,128)(2,1)S(1)} %bitcast.27), custom_call_target="tpu_custom_call" | custom-call | tf_op jit(solution)/shard_map/unpack/pallas_call | solution.py:508
Async XLA Ops:
  1.6 0.9 copy-start.3
  2.5 0.9 copy-start.4
  3.4 0.7 copy-start.6
  4.1 0.7 copy-start.9
  4.8 0.7 copy-start.10
  7.8 1.3 %copy-start = (bf16[1024,544]{0,1:T(8,128)(2,1)S(1)}, bf16[1024,544]{0,1:T(8,128)(2,1)}, u32[]{:S(2)}) copy-start(bf16[1024,544]{0,1:T(8,128)(2,1)} %param.19) | copy-start | bytes 3342340
  9.1 1.2 %copy-start.1 = (bf16[512,1024]{1,0:T(8,128)(2,1)S(1)}, bf16[512,1024]{1,0:T(8,128)(2,1)}, u32[]{:S(2)}) copy-start(bf16[512,1024]{1,0:T(8,128)(2,1)} %dtproj_in.1) | copy-start | bytes 3145732
  10.3 1.2 %copy-start.2 = (f32[16,16,1024]{2,1,0:T(8,128)S(1)}, f32[16,16,1024]{2,1,0:T(8,128)}, u32[]{:S(2)}) copy-start(f32[16,16,1024]{2,1,0:T(8,128)} %state_in.1) | copy-start | bytes 3145732
  11.5 0.8 copy-start.5
  12.4 0.7 copy-start.7
  13.0 0.7 copy-start.8

commit v5 on v4

--- a/solution.py
+++ b/solution.py
@@ -8,6 +8,7 @@
 MESH = pl.DeviceIdType.MESH
 SIDE = 8
 NEAR_FIRST = (1, 7, 2, 6, 3, 5, 4)
+BLOCK_HOPS = (1, 2, 3, -1, -2)
 
 
 def swap_matrix(first, second):
@@ -156,12 +157,13 @@
         scratch_shapes=[pltpu.VMEM(array.shape, array.dtype) for array in arrays]
         + [pltpu.SemaphoreType.DMA((3,))],
         name="attention",
-        compiler_params=pltpu.CompilerParams(vmem_limit_bytes=32 << 20),
+        compiler_params=pltpu.CompilerParams(vmem_limit_bytes=60 << 20),
     )(lengths, destination, *arrays)
 
 
 def move_kernel(
     chosen,
+    table,
     early,
     mamba_in,
     xproj_in,
@@ -188,30 +190,37 @@
     b_wide,
     c_wide,
     readout,
-    moved_state,
-    late_mixed,
-    placed_early,
-    placed_late,
-    middle_early,
-    middle_late,
+    late,
+    bundles_early,
+    bundles_late,
+    tables_come,
+    tables,
     loaded,
     sum_sent,
     sum_come,
     total_sent,
     total_come,
+    table_sent,
+    table_come,
+    table_kept,
     first_sent,
     first_come,
     sent,
     come,
     kept,
+    *blocks,
 ):
     me = lax.axis_index("replica")
     shard = lax.axis_index("tensor")
     shards = lax.axis_size("tensor")
     place = (me // SIDE, me % SIDE)
+    ahead = 1 - 2 * lax.rem(shard, 2)
 
     def device(route, first, second):
         return (first * SIDE + second if route == 0 else second * SIDE + first, shard)
+
+    def along(route, hop):
+        return lax.rem(place[route] + hop * ahead + SIDE, SIDE)
 
     barrier = pltpu.get_barrier_semaphore()
     for hop in range(1, shards):
@@ -239,63 +248,162 @@
     for load in loads:
         load.start()
 
-    def put_early(index, unused):
-        first, second = index // SIDE, index % SIDE
-        placed_early[0, first, second] = early[0, chosen[first * SIDE + second]]
-        placed_early[1, first, second] = early[1, chosen[second * SIDE + first]]
-        return unused
-
-    stages = ((placed_early, middle_early, out_early), (placed_late, middle_late, out_late))
-    first_copies = {}
-
-    def send_first(stage):
-        placed, middle, _ = stages[stage]
-        for hop in NEAR_FIRST:
-            for route in range(2):
-                target = lax.rem(place[route] + hop, SIDE)
-                copy = pltpu.make_async_remote_copy(
-                    src_ref=placed.at[route, target],
-                    dst_ref=middle.at[route, hop],
-                    send_sem=first_sent.at[stage, route, hop],
-                    recv_sem=first_come.at[stage, route, hop],
-                    device_id=device(route, target, place[1 - route]),
-                    device_id_type=MESH,
-                )
-                copy.start()
-                first_copies[stage, route, hop] = copy
-
-    def pass_on(stage, route, bundle, origin):
+    steps, _, rows, width = mamba.shape
+    sources = (early, late)
+    bundles = (bundles_early, bundles_late)
+    outs = (out_early, out_late)
+    hops = len(BLOCK_HOPS)
+
+    def block_of(stage, route, which):
+        return blocks[(stage * 2 + route) * hops + which]
+
+    for stage in range(2):
+        for route in range(2):
+            for which in range(hops):
+                block = block_of(stage, route, which)
+                block[rows] = jnp.zeros(block.shape[1:], block.dtype)
+    for route in range(2):
+        late[route, rows] = jnp.zeros(late.shape[2:], late.dtype)
+
+    started = []
+
+    def ship(source, target, stage, route, which, step):
+        copy = pltpu.make_async_remote_copy(
+            src_ref=source,
+            dst_ref=target,
+            send_sem=first_sent.at[stage, route, which],
+            recv_sem=first_come.at[stage, route, which],
+            device_id=device(route, along(route, step), place[1 - route]),
+            device_id_type=MESH,
+        )
+        copy.start()
+        started.append(copy)
+        return copy
+
+    def select(stage, route, block, slots, first, kind):
+        def one(second, unused):
+            slot = first * SIDE + second if route == 0 else second * SIDE + first
+            bundles[stage][route, kind, second] = block[slots(slot)]
+            return unused
+
+        lax.fori_loop(0, SIDE, one, 0)
+
+    def pass_on(stage, route, kind, hop):
         mine = place[1 - route]
-        out = stages[stage][2]
+        origin = along(route, -hop)
         pair = (origin, mine) if route == 0 else (mine, origin)
-        slot = out.at[route, pair[0], pair[1]]
-        for hop in NEAR_FIRST:
-            target = lax.rem(mine + hop, SIDE)
+        slot = outs[stage].at[route, pair[0], pair[1]]
+        for step in NEAR_FIRST:
+            target = lax.rem(mine + step, SIDE)
             pltpu.make_async_remote_copy(
-                src_ref=bundle.at[target],
+                src_ref=bundles[stage].at[route, kind, target],
                 dst_ref=slot,
                 send_sem=sent.at[stage],
                 recv_sem=come.at[stage],
                 device_id=device(route, place[route], target),
                 device_id_type=MESH,
             ).start()
-        pltpu.make_async_copy(bundle.at[mine], slot, kept.at[stage]).start()
+        pltpu.make_async_copy(
+            bundles[stage].at[route, kind, mine], slot, kept.at[stage]
+        ).start()
 
     def pass_own(stage):
         for route in range(2):
-            pass_on(stage, route, stages[stage][0].at[route, place[route]], place[route])
-
-    def pass_arrived(stage):
-        for hop in NEAR_FIRST:
-            for route in range(2):
-                first_copies[stage, route, hop].wait_recv()
-                origin = lax.rem(place[route] + SIDE - hop, SIDE)
-                pass_on(stage, route, stages[stage][1].at[route, hop], origin)
-
-    lax.fori_loop(0, SIDE * SIDE, put_early, 0)
+            block = sources[stage].at[route]
+            select(stage, route, block, lambda slot: chosen[slot], place[route], 0)
+            pass_on(stage, route, 0, 0)
+
+    def pass_block(stage, route, which):
+        select(
+            stage,
+            route,
+            block_of(stage, route, which),
+            lambda slot: tables[route, which, 0, slot],
+            place[route],
+            1 + which,
+        )
+        pass_on(stage, route, 1 + which, BLOCK_HOPS[which])
+
+    legs = {}
+
+    def start_block(stage, route, which, source, step):
+        target = block_of(stage, route, which).at[pl.ds(0, rows)]
+        legs[stage, route, which] = ship(
+            source.at[pl.ds(0, rows)], target, stage, route, which, step
+        )
+
+    def start_bundle(stage, route, which, kind, step):
+        select(
+            stage,
+            route,
+            block_of(stage, route, which),
+            lambda slot: tables[route, which, 0, slot],
+            along(route, step),
+            kind,
+        )
+        held = bundles[stage]
+        legs[stage, route, kind] = ship(
+            held.at[route, kind], held.at[route, kind + 2], stage, route, kind, step
+        )
+
+    def first_leg(stage):
+        for route in range(2):
+            start_block(stage, route, 0, sources[stage].at[route], 1)
+            start_block(stage, route, 3, sources[stage].at[route], -1)
+
+    def second_leg(stage):
+        for route in range(2):
+            legs[stage, route, 0].wait_recv()
+            start_block(stage, route, 1, block_of(stage, route, 0), 1)
+            legs[stage, route, 3].wait_recv()
+            start_block(stage, route, 4, block_of(stage, route, 3), -1)
+        for route in range(2):
+            pass_block(stage, route, 0)
+            pass_block(stage, route, 3)
+
+    def third_leg(stage):
+        for route in range(2):
+            legs[stage, route, 1].wait_recv()
+            start_block(stage, route, 2, block_of(stage, route, 1), 1)
+            legs[stage, route, 4].wait_recv()
+            start_bundle(stage, route, 4, 6, -1)
+        for route in range(2):
+            pass_block(stage, route, 1)
+            pass_block(stage, route, 4)
+
+    def fourth_leg(stage):
+        for route in range(2):
+            legs[stage, route, 2].wait_recv()
+            start_bundle(stage, route, 2, 7, 1)
+        for route in range(2):
+            pass_block(stage, route, 2)
+            legs[stage, route, 6].wait_recv()
+            pass_on(stage, route, 8, -3)
+
+    def last_leg(stage):
+        for route in range(2):
+            legs[stage, route, 7].wait_recv()
+            pass_on(stage, route, 9, 4)
+
+    pl.semaphore_wait(barrier, shards - 1 + 2 * len(NEAR_FIRST))
+    table_legs = []
+    for which, hop in enumerate(BLOCK_HOPS):
+        for route in range(2):
+            copy = pltpu.make_async_remote_copy(
+                src_ref=table,
+                dst_ref=tables_come.at[route, which],
+                send_sem=table_sent.at[route, which],
+                recv_sem=table_come.at[route, which],
+                device_id=device(route, along(route, hop), place[1 - route]),
+                device_id_type=MESH,
+            )
+            copy.start()
+            table_legs.append(copy)
+    first_leg(0)
+    pass_own(0)
+
     loads[0].wait()
     loads[1].wait()
-    steps, _, rows, width = mamba.shape
     chunk = part.shape[1]
     per_step = rows // chunk
     for step in range(steps):
@@ -309,8 +417,6 @@
             part[step * per_step + piece] = block[piece * chunk : (piece + 1) * chunk]
     for piece in range(steps * per_step, shards):
         part[piece] = jnp.zeros(part.shape[1:], part.dtype)
-    pl.semaphore_wait(barrier, shards - 1 + 2 * len(NEAR_FIRST))
-
     sums = []
     for hop in range(1, shards):
         target = lax.rem(shard + hop, shards)
@@ -324,13 +430,14 @@
         )
         copy.start()
         sums.append(copy)
-    send_first(0)
-    pass_own(0)
+    for copy in table_legs:
+        copy.wait_recv()
+    keep = pltpu.make_async_copy(tables_come, tables, table_kept)
+    keep.start()
+    keep.wait()
     for load in loads[2:]:
         load.wait()
     decay_rate[...] = -jnp.exp(a_log[...])
-    moved_state[rows] = jnp.zeros(moved_state.shape[1:], moved_state.dtype)
-    late_mixed[rows] = jnp.zeros(late_mixed.shape[1:], late_mixed.dtype)
 
     summed = part[shard]
     for hop in range(1, shards):
@@ -350,6 +457,7 @@
         )
         copy.start()
         totals.append(copy)
+    second_leg(0)
     for copy in totals:
         copy.wait_recv()
 
@@ -369,60 +477,61 @@
         b_wide[index] = jnp.broadcast_to(column[:state_size], (state_size, lane))
         c_wide[index] = jnp.broadcast_to(column[state_size:], (state_size, lane))
 
-    cut = placed_late.shape[4]
+    cut = late.shape[3]
     rest = width - cut
 
-    def update(piece, unused):
-        span = pl.ds(pl.multiple_of(piece * lane, lane), lane)
-        rate = decay_rate[:, span]
-        for row in range(rows):
-            carry = state[row, :, span]
-            for step in range(steps):
-                index = step * rows + row
-                size = step_size[index : index + 1, span]
-                carry = (
-                    jnp.exp(size * rate) * carry
-                    + b_wide[index] * drive[index : index + 1, span]
-                )
-                readout[index : index + 1, span] = jnp.sum(
-                    c_wide[index] * carry, axis=0, keepdims=True
-                )
-            moved_state[row, :, span] = carry.astype(jnp.bfloat16)
-        return unused
-
-    lax.fori_loop(0, width // lane, update, 0)
+    def update(route, skipped):
+        def one(piece, unused):
+            span = pl.ds(pl.multiple_of(piece * lane + skipped, lane), lane)
+            goal = pl.ds(pl.multiple_of(piece * lane, lane), lane)
+            rate = decay_rate[:, span]
+            for row in range(rows):
+                carry = state[row, :, span]
+                for step in range(steps):
+                    index = step * rows + row
+                    size = step_size[index : index + 1, span]
+                    carry = (
+                        jnp.exp(size * rate) * carry
+                        + b_wide[index] * drive[index : index + 1, span]
+                    )
+                    readout[index : index + 1, span] = jnp.sum(
+                        c_wide[index] * carry, axis=0, keepdims=True
+                    )
+                late[route, row, :, goal] = carry.astype(jnp.bfloat16)
+            return unused
+
+        return one
+
+    lax.fori_loop(0, cut // lane, update(0, 0), 0)
+    lax.fori_loop(0, rest // lane, update(1, cut), 0)
     page_width = cut - rest
-    blocks = []
+    pieces = []
     for step in range(steps):
         x = mamba[step, 0].astype(jnp.float32)
         z = mamba[step, 1].astype(jnp.float32)
         whole = readout[step * rows : (step + 1) * rows] + skip[...] * x
         mixed = (whole * (z / (1.0 + jnp.exp(-z)))).astype(jnp.bfloat16)
         for start in range(0, width, page_width):
-            blocks.append(mixed[:, start : start + page_width])
-    while len(blocks) < state_size:
-        blocks.append(jnp.zeros((rows, page_width), jnp.bfloat16))
-    late_mixed[:rows] = swap_rows(jnp.stack(blocks))
-
-    def put_late(index, unused):
-        first, second = index // SIDE, index % SIDE
-        placed_late[0, first, second] = moved_state[chosen[first * SIDE + second], :, :cut]
-        row = chosen[second * SIDE + first]
-        placed_late[1, first, second, :, :rest] = moved_state[row, :, cut:]
-        placed_late[1, first, second, :, rest:] = late_mixed[row]
-        return unused
-
-    lax.fori_loop(0, SIDE * SIDE, put_late, 0)
-    send_first(1)
+            pieces.append(mixed[:, start : start + page_width])
+    while len(pieces) < state_size:
+        pieces.append(jnp.zeros((rows, page_width), jnp.bfloat16))
+    late[1, :rows, :, rest:] = swap_rows(jnp.stack(pieces))
+
+    first_leg(1)
+    third_leg(0)
     pass_own(1)
-    pass_arrived(0)
-    pass_arrived(1)
-    for copy in sums + totals + list(first_copies.values()):
+    fourth_leg(0)
+    second_leg(1)
+    last_leg(0)
+    third_leg(1)
+    fourth_leg(1)
+    last_leg(1)
+
+    for copy in table_legs + sums + totals + started:
         copy.wait_send()
     for stage in range(2):
-        out = stages[stage][2]
-        others = out.at[:, :, pl.ds(0, SIDE - 1)]
-        own = out.at[:, :, 0]
+        others = outs[stage].at[:, :, pl.ds(0, SIDE - 1)]
+        own = outs[stage].at[:, :, 0]
         pltpu.make_async_copy(own, own, kept.at[stage]).wait()
         pltpu.make_async_copy(others, others, sent.at[stage]).wait()
         pltpu.make_async_copy(others, others, come.at[stage]).wait()
@@ -436,8 +545,13 @@
     shards = lax.axis_size("tensor")
     arrays = (mamba, xproj_w, dtproj_w, dt_bias, a_log, d_skip, state)
     grid = (2, SIDE, SIDE, state_size)
+    kinds = (2, 10, SIDE, state_size)
     early_grid, late_grid = grid + (page_width,), grid + (half,)
     sums = (shards, steps * rows // 6, xproj_w.shape[0])
+    tables = (2, len(BLOCK_HOPS), 1, chosen.shape[0])
+    early_block = pltpu.VMEM((rows + 1, state_size, page_width), jnp.bfloat16)
+    late_block = pltpu.VMEM((rows + 1, state_size, half), jnp.bfloat16)
+    blocks = [early_block] * (2 * len(BLOCK_HOPS)) + [late_block] * (2 * len(BLOCK_HOPS))
     outs = pl.pallas_call(
         move_kernel,
         out_shape=(
@@ -446,6 +560,7 @@
         ),
         in_specs=[
             pl.BlockSpec(memory_space=pltpu.SMEM),
+            pl.BlockSpec(memory_space=pltpu.VMEM),
             pl.BlockSpec(memory_space=pltpu.VMEM),
         ]
         + [pl.BlockSpec(memory_space=pl.ANY)] * len(arrays),
@@ -459,22 +574,24 @@
             pltpu.VMEM((steps * rows, state_size, 128), jnp.float32),
             pltpu.VMEM((steps * rows, state_size, 128), jnp.float32),
             pltpu.VMEM((steps * rows, width), jnp.float32),
-            pltpu.VMEM((rows + 1, state_size, width), jnp.bfloat16),
-            pltpu.VMEM((rows + 1, state_size, page_width), jnp.bfloat16),
-            pltpu.VMEM(early_grid, jnp.bfloat16),
-            pltpu.VMEM(late_grid, jnp.bfloat16),
-            pltpu.VMEM(early_grid, jnp.bfloat16),
-            pltpu.VMEM(late_grid, jnp.bfloat16),
+            pltpu.VMEM((2, rows + 1, state_size, half), jnp.bfloat16),
+            pltpu.VMEM(kinds + (page_width,), jnp.bfloat16),
+            pltpu.VMEM(kinds + (half,), jnp.bfloat16),
+            pltpu.VMEM(tables, jnp.int32),
+            pltpu.SMEM(tables, jnp.int32),
             pltpu.SemaphoreType.DMA((len(arrays),)),
         ]
         + [pltpu.SemaphoreType.DMA((shards,))] * 4
+        + [pltpu.SemaphoreType.DMA((2, len(BLOCK_HOPS)))] * 2
+        + [pltpu.SemaphoreType.DMA]
         + [pltpu.SemaphoreType.DMA((2, 2, SIDE))] * 2
-        + [pltpu.SemaphoreType.DMA((2,))] * 3,
+        + [pltpu.SemaphoreType.DMA((2,))] * 3
+        + blocks,
         name="move_rows",
         compiler_params=pltpu.CompilerParams(
-            collective_id=1, has_side_effects=True, vmem_limit_bytes=32 << 20
+            collective_id=1, has_side_effects=True, vmem_limit_bytes=60 << 20
         ),
-    )(chosen, early, *arrays)
+    )(chosen, chosen[None], early, *arrays)
     return [out.reshape((2, SIDE * SIDE) + out.shape[3:]) for out in outs]
 
 
@@ -525,7 +642,7 @@
             pl.BlockSpec((state_size + steps, block, page_width), lambda i: (0, i, 0)),
         ),
         name="unpack",
-        compiler_params=pltpu.CompilerParams(vmem_limit_bytes=32 << 20),
+        compiler_params=pltpu.CompilerParams(vmem_limit_bytes=60 << 20),
     )(early, late)
 
 
@@ -550,7 +667,7 @@
         kv_cache[:, :, 0],
         lengths,
         destination[:, 0],
-        lax.axis_size("replica"),
+        2 * lax.axis_size("replica"),
         a_log.shape[0],
     )
     early, late = move_rows(

time: 115 us -> 101 us (0.88)
  local copies, waits for them, and re-layouts: 10.7 us -> 1.64 us
  Pallas kernels: 102 us -> 97.1 us
    unnamed x23 -> x1, local copies, waits for them, and re-layouts: 10.7 us -> 1.64 us
    pallas_call x1, Pallas kernels: 96.3 us -> 88.9 us  [move_rows(): pl.pallas_call(move_kernel, out_shape=(jax.ShapeDtypeStruct(early_grid, j...]
    pallas_call x1, Pallas kernels: 2.94 us -> 4.88 us  [unpack(): pl.pallas_call(unpack_kernel, grid=(slots // block,), out_shape=(jax.Shap...]
where the time goes in v5:
time: 101 us; the launch traced here: 99.4 us
  Pallas kernels  97.1 us (96%)
  local copies, waits for them, and re-layouts  1.64 us (2%)
    pallas_call x1, Pallas kernels, move_rows(): pl.pallas_call(move_kernel, out_shape=(jax.ShapeDtypeStruct(early_grid, j...  88.9 us
    pallas_call x1, Pallas kernels, unpack(): pl.pallas_call(unpack_kernel, grid=(slots // block,), out_shape=(jax.Shap...  4.88 us
    pallas_call x1, Pallas kernels, attention(): pl.pallas_call(attention_kernel, out_shape=(jax.ShapeDtypeStruct((2, rows...  3.28 us

profile of v5, /device:TPU:6, one launch (start us, length us, event | category | flops | bytes accessed | tf_op | source)
XLA Modules:
  0.0 99.4 jit_solution(6834395636004057257)
XLA Ops:
  0.6 1.6 %copy.20 = bf16[16,3,2,1024]{3,0,2,1:T(8,128)(2,1)} copy(bf16[16,3,2,1024]{3,2,1,0:T(2,128)(2,1)} %param.12) | data formatting | bytes 393216 | tf_op args[0]
  2.3 3.3 %attention.1 = (bf16[2,17,16,256]{3,2,1,0:T(8,128)(2,1)}, s32[128]{0:T(128)}) custom-call(s32[16]{0:T(128)} %lengths.1, s32[16]{0:T(128)} %bitcast.38, bf16[3,16,1024]{2,1,0:T(8,128)(2,1)} %bitcast.33, bf16[3,16,256]{2,1,0:T(8,128)(2,1)} %bitcast.34, bf16[16,16,256]{2,1,0:T(8,128)(2,1)} %bitcast.32), custom_call_target="tpu_custom_call" | custom-call | tf_op jit(solution)/shard_map/attention/pallas_call | solution.py:145
  5.6 88.9 %move_rows.1 = (bf16[2,8,8,16,256]{4,3,2,1,0:T(8,128)(2,1)}, bf16[2,8,8,16,640]{4,3,2,1,0:T(8,128)(2,1)}) custom-call(s32[128]{0:T(128)} %get-tuple-element.12.chosen, s32[1,128]{1,0:T(1,128)} %bitcast.37, bf16[2,17,16,256]{3,2,1,0:T(8,128)(2,1)} %get-tuple-element.13.early, bf16[3,2,16,1024]{3,2,1,0:T(8,128)(2,1)} %bitcast.31, bf16[544,1024]{1,0:T(8,128)(2,1)} %bitcast.29, ...), custom_call_target="tpu_custom_call" | custom-call | tf_op jit(solution)/shard_map/move_rows/pallas_call | solution.py:555
  94.5 4.9 %unpack.1 = (bf16[3,64,1024]{2,1,0:T(8,128)(2,1)}, bf16[3,64,1024]{2,1,0:T(8,128)(2,1)}, bf16[64,16,1024]{2,1,0:T(8,128)(2,1)}, bf16[19,64,256]{2,1,0:T(8,128)(2,1)}) custom-call(bf16[2,64,16,256]{3,2,1,0:T(8,128)(2,1)} %bitcast.30, bf16[2,64,16,640]{3,2,1,0:T(8,128)(2,1)} %bitcast.28), custom_call_target="tpu_custom_call" | custom-call | tf_op jit(solution)/shard_map/unpack/pallas_call | solution.py:625

commit v6 on v5

--- a/solution.py
+++ b/solution.py
@@ -88,85 +88,14 @@
     return grown.reshape(rows, context, width), tail.astype(jnp.bfloat16).reshape(steps, rows, width)
 
 
-def attention_kernel(
-    lengths, destination, queries_in, fresh_in, cached_in, packed, chosen, queries, fresh, cached, come
-):
-    copies = [
-        pltpu.make_async_copy(source, held, come.at[index])
-        for index, (source, held) in enumerate(
-            [(queries_in, queries), (fresh_in, fresh), (cached_in, cached)]
-        )
-    ]
-    for copy in copies:
-        copy.start()
-    rows, context, page_width = cached.shape
-    steps = queries.shape[0]
-    state_size = packed.shape[2]
-
-    def clear(slot, carry):
-        chosen[slot] = rows
-        return carry
-
-    def choose(row, carry):
-        chosen[destination[row]] = row
-        return carry
-
-    lax.fori_loop(0, chosen.shape[0], clear, 0)
-    lax.fori_loop(0, rows, choose, 0)
-
-    token = lax.broadcasted_iota(jnp.int32, (1, steps * rows), 1)
-    asked = lax.broadcasted_iota(jnp.int32, (1, rows * context + steps * rows), 1)
-    key_row = jnp.where(asked < rows * context, asked // context, (asked - rows * context) % rows)
-    key_lengths = jnp.zeros_like(asked)
-    token_lengths = jnp.zeros_like(token)
-    for row in range(rows):
-        key_lengths = jnp.where(key_row == row, lengths[row], key_lengths)
-        token_lengths = jnp.where(token % rows == row, lengths[row], token_lengths)
-    for copy in copies:
-        copy.wait()
-    grown, tail = grow(cached[...], fresh[...], token_lengths)
-    packed[0, :rows] = grown
-    attended = attend(queries[...], cached[...], fresh[...], key_lengths)
-    per_block = page_width // 128
-    blocks = [tail[s] for s in range(steps)]
-    for step in range(steps):
-        for g in range(0, len(attended[step]), per_block):
-            blocks.append(jnp.concatenate(attended[step][g : g + per_block], axis=1))
-    while len(blocks) < state_size:
-        blocks.append(jnp.zeros((rows, page_width), jnp.bfloat16))
-    packed[1, :rows] = swap_rows(jnp.stack(blocks))
-    packed[0, rows] = jnp.zeros(packed.shape[2:], packed.dtype)
-    packed[1, rows] = jnp.zeros(packed.shape[2:], packed.dtype)
-
-
-def attention(queries, fresh, cached, lengths, destination, slots, state_size):
-    rows, _, page_width = cached.shape
-    arrays = (queries, fresh, cached)
-    return pl.pallas_call(
-        attention_kernel,
-        out_shape=(
-            jax.ShapeDtypeStruct((2, rows + 1, state_size, page_width), jnp.bfloat16),
-            jax.ShapeDtypeStruct((slots,), jnp.int32),
-        ),
-        in_specs=[pl.BlockSpec(memory_space=pltpu.SMEM)] * 2
-        + [pl.BlockSpec(memory_space=pl.ANY)] * 3,
-        out_specs=(
-            pl.BlockSpec(memory_space=pltpu.VMEM),
-            pl.BlockSpec(memory_space=pltpu.SMEM),
-        ),
-        scratch_shapes=[pltpu.VMEM(array.shape, array.dtype) for array in arrays]
-        + [pltpu.SemaphoreType.DMA((3,))],
-        name="attention",
-        compiler_params=pltpu.CompilerParams(vmem_limit_bytes=60 << 20),
-    )(lengths, destination, *arrays)
-
-
 def move_kernel(
-    chosen,
-    table,
-    early,
+    lengths,
+    destination,
     mamba_in,
     xproj_in,
+    cached_in,
+    fresh_in,
+    queries_in,
     dtproj_in,
     bias_in,
     a_log_in,
@@ -176,6 +105,9 @@
     out_late,
     mamba,
     xproj,
+    cached,
+    fresh,
+    queries,
     dtproj,
     bias,
     a_log,
@@ -190,9 +122,12 @@
     b_wide,
     c_wide,
     readout,
+    early,
     late,
     bundles_early,
     bundles_late,
+    table,
+    chosen,
     tables_come,
     tables,
     loaded,
@@ -237,6 +172,9 @@
             [
                 (mamba_in, mamba),
                 (xproj_in, xproj),
+                (cached_in, cached),
+                (fresh_in, fresh),
+                (queries_in, queries),
                 (dtproj_in, dtproj),
                 (bias_in, bias),
                 (a_log_in, a_log),
@@ -263,7 +201,15 @@
                 block = block_of(stage, route, which)
                 block[rows] = jnp.zeros(block.shape[1:], block.dtype)
     for route in range(2):
+        early[route, rows] = jnp.zeros(early.shape[2:], early.dtype)
         late[route, rows] = jnp.zeros(late.shape[2:], late.dtype)
+    slot_id = lax.broadcasted_iota(jnp.int32, table.shape, 1)
+    slot_row = jnp.full(table.shape, rows, jnp.int32)
+    for row in range(rows):
+        slot_row = jnp.where(slot_id == destination[row], row, slot_row)
+    table[...] = slot_row
+    keep_own = pltpu.make_async_copy(table, chosen, table_kept.at[0])
+    keep_own.start()
 
     started = []
 
@@ -310,7 +256,7 @@
     def pass_own(stage):
         for route in range(2):
             block = sources[stage].at[route]
-            select(stage, route, block, lambda slot: chosen[slot], place[route], 0)
+            select(stage, route, block, lambda slot: chosen[0, slot], place[route], 0)
             pass_on(stage, route, 0, 0)
 
     def pass_block(stage, route, which):
@@ -346,10 +292,9 @@
             held.at[route, kind], held.at[route, kind + 2], stage, route, kind, step
         )
 
-    def first_leg(stage):
-        for route in range(2):
-            start_block(stage, route, 0, sources[stage].at[route], 1)
-            start_block(stage, route, 3, sources[stage].at[route], -1)
+    def first_leg(stage, route):
+        start_block(stage, route, 0, sources[stage].at[route], 1)
+        start_block(stage, route, 3, sources[stage].at[route], -1)
 
     def second_leg(stage):
         for route in range(2):
@@ -385,7 +330,37 @@
             legs[stage, route, 7].wait_recv()
             pass_on(stage, route, 9, 4)
 
+    loads[0].wait()
+    loads[1].wait()
+    chunk = part.shape[1]
+    per_step = rows // chunk
+    for step in range(steps):
+        block = lax.dot_general(
+            mamba[step, 0],
+            xproj[...],
+            (((1,), (1,)), ((), ())),
+            preferred_element_type=jnp.float32,
+        )
+        for piece in range(per_step):
+            part[step * per_step + piece] = block[piece * chunk : (piece + 1) * chunk]
+    for piece in range(steps * per_step, shards):
+        part[piece] = jnp.zeros(part.shape[1:], part.dtype)
+    keep_own.wait()
     pl.semaphore_wait(barrier, shards - 1 + 2 * len(NEAR_FIRST))
+
+    sums = []
+    for hop in range(1, shards):
+        target = lax.rem(shard + hop, shards)
+        copy = pltpu.make_async_remote_copy(
+            src_ref=part.at[target],
+            dst_ref=arrived.at[hop],
+            send_sem=sum_sent.at[hop],
+            recv_sem=sum_come.at[hop],
+            device_id=(me, target),
+            device_id_type=MESH,
+        )
+        copy.start()
+        sums.append(copy)
     table_legs = []
     for which, hop in enumerate(BLOCK_HOPS):
         for route in range(2):
@@ -399,43 +374,33 @@
             )
             copy.start()
             table_legs.append(copy)
-    first_leg(0)
+
+    context, page_width = cached.shape[1:]
+    token = lax.broadcasted_iota(jnp.int32, (1, steps * rows), 1)
+    asked = lax.broadcasted_iota(jnp.int32, (1, rows * context + steps * rows), 1)
+    key_row = jnp.where(asked < rows * context, asked // context, (asked - rows * context) % rows)
+    key_lengths = jnp.zeros_like(asked)
+    token_lengths = jnp.zeros_like(token)
+    for row in range(rows):
+        key_lengths = jnp.where(key_row == row, lengths[row], key_lengths)
+        token_lengths = jnp.where(token % rows == row, lengths[row], token_lengths)
+    for load in loads[2:5]:
+        load.wait()
+    grown, tail = grow(cached[...], fresh[...], token_lengths)
+    early[0, :rows] = grown
+    first_leg(0, 0)
+    attended = attend(queries[...], cached[...], fresh[...], key_lengths)
+    per_block = page_width // 128
+    pieces = [tail[step] for step in range(steps)]
+    for step in range(steps):
+        for g in range(0, len(attended[step]), per_block):
+            pieces.append(jnp.concatenate(attended[step][g : g + per_block], axis=1))
+    while len(pieces) < early.shape[2]:
+        pieces.append(jnp.zeros((rows, page_width), jnp.bfloat16))
+    early[1, :rows] = swap_rows(jnp.stack(pieces))
+    first_leg(0, 1)
     pass_own(0)
-
-    loads[0].wait()
-    loads[1].wait()
-    chunk = part.shape[1]
-    per_step = rows // chunk
-    for step in range(steps):
-        block = lax.dot_general(
-            mamba[step, 0],
-            xproj[...],
-            (((1,), (1,)), ((), ())),
-            preferred_element_type=jnp.float32,
-        )
-        for piece in range(per_step):
-            part[step * per_step + piece] = block[piece * chunk : (piece + 1) * chunk]
-    for piece in range(steps * per_step, shards):
-        part[piece] = jnp.zeros(part.shape[1:], part.dtype)
-    sums = []
-    for hop in range(1, shards):
-        target = lax.rem(shard + hop, shards)
-        copy = pltpu.make_async_remote_copy(
-            src_ref=part.at[target],
-            dst_ref=arrived.at[hop],
-            send_sem=sum_sent.at[hop],
-            recv_sem=sum_come.at[hop],
-            device_id=(me, target),
-            device_id_type=MESH,
-        )
-        copy.start()
-        sums.append(copy)
-    for copy in table_legs:
-        copy.wait_recv()
-    keep = pltpu.make_async_copy(tables_come, tables, table_kept)
-    keep.start()
-    keep.wait()
-    for load in loads[2:]:
+    for load in loads[5:]:
         load.wait()
     decay_rate[...] = -jnp.exp(a_log[...])
 
@@ -457,6 +422,11 @@
         )
         copy.start()
         totals.append(copy)
+    for copy in table_legs:
+        copy.wait_recv()
+    keep = pltpu.make_async_copy(tables_come, tables, table_kept.at[1])
+    keep.start()
+    keep.wait()
     second_leg(0)
     for copy in totals:
         copy.wait_recv()
@@ -502,9 +472,10 @@
 
         return one
 
+    third_leg(0)
     lax.fori_loop(0, cut // lane, update(0, 0), 0)
+    first_leg(1, 0)
     lax.fori_loop(0, rest // lane, update(1, cut), 0)
-    page_width = cut - rest
     pieces = []
     for step in range(steps):
         x = mamba[step, 0].astype(jnp.float32)
@@ -517,8 +488,7 @@
         pieces.append(jnp.zeros((rows, page_width), jnp.bfloat16))
     late[1, :rows, :, rest:] = swap_rows(jnp.stack(pieces))
 
-    first_leg(1)
-    third_leg(0)
+    first_leg(1, 1)
     pass_own(1)
     fourth_leg(0)
     second_leg(1)
@@ -537,18 +507,19 @@
         pltpu.make_async_copy(others, others, come.at[stage]).wait()
 
 
-def move_rows(chosen, early, mamba, xproj_w, dtproj_w, dt_bias, a_log, d_skip, state):
+def move_rows(lengths, destination, *arrays):
+    mamba, xproj_w, cached, a_log = arrays[0], arrays[1], arrays[2], arrays[7]
     steps, _, rows, width = mamba.shape
     state_size = a_log.shape[0]
-    page_width = early.shape[3]
+    page_width = cached.shape[2]
     half = (width + page_width) // 2
     shards = lax.axis_size("tensor")
-    arrays = (mamba, xproj_w, dtproj_w, dt_bias, a_log, d_skip, state)
     grid = (2, SIDE, SIDE, state_size)
     kinds = (2, 10, SIDE, state_size)
     early_grid, late_grid = grid + (page_width,), grid + (half,)
     sums = (shards, steps * rows // 6, xproj_w.shape[0])
-    tables = (2, len(BLOCK_HOPS), 1, chosen.shape[0])
+    table = (1, 2 * SIDE * SIDE)
+    tables = (2, len(BLOCK_HOPS)) + table
     early_block = pltpu.VMEM((rows + 1, state_size, page_width), jnp.bfloat16)
     late_block = pltpu.VMEM((rows + 1, state_size, half), jnp.bfloat16)
     blocks = [early_block] * (2 * len(BLOCK_HOPS)) + [late_block] * (2 * len(BLOCK_HOPS))
@@ -560,8 +531,7 @@
         ),
         in_specs=[
             pl.BlockSpec(memory_space=pltpu.SMEM),
-            pl.BlockSpec(memory_space=pltpu.VMEM),
-            pl.BlockSpec(memory_space=pltpu.VMEM),
+            pl.BlockSpec(memory_space=pltpu.SMEM),
         ]
         + [pl.BlockSpec(memory_space=pl.ANY)] * len(arrays),
         out_specs=(pl.BlockSpec(memory_space=pl.ANY), pl.BlockSpec(memory_space=pl.ANY)),
@@ -574,16 +544,19 @@
             pltpu.VMEM((steps * rows, state_size, 128), jnp.float32),
             pltpu.VMEM((steps * rows, state_size, 128), jnp.float32),
             pltpu.VMEM((steps * rows, width), jnp.float32),
+            pltpu.VMEM((2, rows + 1, state_size, page_width), jnp.bfloat16),
             pltpu.VMEM((2, rows + 1, state_size, half), jnp.bfloat16),
             pltpu.VMEM(kinds + (page_width,), jnp.bfloat16),
             pltpu.VMEM(kinds + (half,), jnp.bfloat16),
+            pltpu.VMEM(table, jnp.int32),
+            pltpu.SMEM(table, jnp.int32),
             pltpu.VMEM(tables, jnp.int32),
             pltpu.SMEM(tables, jnp.int32),
             pltpu.SemaphoreType.DMA((len(arrays),)),
         ]
         + [pltpu.SemaphoreType.DMA((shards,))] * 4
         + [pltpu.SemaphoreType.DMA((2, len(BLOCK_HOPS)))] * 2
-        + [pltpu.SemaphoreType.DMA]
+        + [pltpu.SemaphoreType.DMA((2,))]
         + [pltpu.SemaphoreType.DMA((2, 2, SIDE))] * 2
         + [pltpu.SemaphoreType.DMA((2,))] * 3
         + blocks,
@@ -591,56 +564,102 @@
         compiler_params=pltpu.CompilerParams(
             collective_id=1, has_side_effects=True, vmem_limit_bytes=60 << 20
         ),
-    )(chosen, chosen[None], early, *arrays)
+    )(lengths, destination, *arrays)
     return [out.reshape((2, SIDE * SIDE) + out.shape[3:]) for out in outs]
 
 
-def unpack_kernel(early, late, mixed, attended, state, pages):
-    steps, _, width = mixed.shape
+def unpack_kernel(
+    early_in,
+    late_in,
+    mixed_out,
+    attended_out,
+    state_out,
+    pages_out,
+    early,
+    late,
+    mixed,
+    attended,
+    pages,
+    come,
+    gone,
+):
+    steps, slots, width = mixed.shape
     page_width = pages.shape[2]
     cut = late.shape[3]
     left = width - cut
     context = early.shape[2]
-    state[:, :, :cut] = late[0]
-    state[:, :, cut:] = late[1, :, :, :left]
-    pages[:context] = swap_rows(early[0])
-    swapped = swap_rows(early[1])
-    pages[context:] = swapped[:steps]
     per_step = width // page_width
-    for step in range(steps):
-        for piece in range(per_step):
-            span = slice(piece * page_width, (piece + 1) * page_width)
-            attended[step, :, span] = swapped[steps + step * per_step + piece]
-    swapped = swap_rows(late[1, :, :, left:])
-    for step in range(steps):
-        for piece in range(per_step):
-            span = slice(piece * page_width, (piece + 1) * page_width)
-            mixed[step, :, span] = swapped[step * per_step + piece]
+    block = 16
+    loads = []
+    for index in range(slots // block):
+        span = pl.ds(index * block, block)
+        group = []
+        for route in range(2):
+            for kind, (source, held) in enumerate([(late_in, late), (early_in, early)]):
+                copy = pltpu.make_async_copy(
+                    source.at[route, span], held.at[route, span], come.at[index, 2 * route + kind]
+                )
+                copy.start()
+                group.append(copy)
+        loads.append(group)
+    stores = []
+
+    def store(source, goal, index, which):
+        copy = pltpu.make_async_copy(source, goal, gone.at[index, which])
+        copy.start()
+        stores.append(copy)
+
+    for index, group in enumerate(loads):
+        for copy in group:
+            copy.wait()
+        span = pl.ds(index * block, block)
+        rows = slice(index * block, (index + 1) * block)
+        store(late.at[0, span], state_out.at[span, :, pl.ds(0, cut)], index, 0)
+        store(
+            late.at[1, span, :, pl.ds(0, left)], state_out.at[span, :, pl.ds(cut, left)], index, 1
+        )
+        pages[:context, rows] = swap_rows(early[0, rows])
+        swapped = swap_rows(early[1, rows])
+        pages[context:, rows] = swapped[:steps]
+        store(pages.at[:, span], pages_out.at[:, span], index, 2)
+        for step in range(steps):
+            for piece in range(per_step):
+                lanes = slice(piece * page_width, (piece + 1) * page_width)
+                attended[step, rows, lanes] = swapped[steps + step * per_step + piece]
+        store(attended.at[:, span], attended_out.at[:, span], index, 3)
+        swapped = swap_rows(late[1, rows, :, left:])
+        for step in range(steps):
+            for piece in range(per_step):
+                lanes = slice(piece * page_width, (piece + 1) * page_width)
+                mixed[step, rows, lanes] = swapped[step * per_step + piece]
+        store(mixed.at[:, span], mixed_out.at[:, span], index, 4)
+    for copy in stores:
+        copy.wait()
 
 
 def unpack(early, late, steps, width):
     _, slots, state_size, page_width = early.shape
-    half = late.shape[3]
-    block = 16
+    wide = (steps, slots, width)
+    paged = (state_size + steps, slots, page_width)
     return pl.pallas_call(
         unpack_kernel,
-        grid=(slots // block,),
         out_shape=(
-            jax.ShapeDtypeStruct((steps, slots, width), jnp.bfloat16),
-            jax.ShapeDtypeStruct((steps, slots, width), jnp.bfloat16),
+            jax.ShapeDtypeStruct(wide, jnp.bfloat16),
+            jax.ShapeDtypeStruct(wide, jnp.bfloat16),
             jax.ShapeDtypeStruct((slots, state_size, width), jnp.bfloat16),
-            jax.ShapeDtypeStruct((state_size + steps, slots, page_width), jnp.bfloat16),
+            jax.ShapeDtypeStruct(paged, jnp.bfloat16),
         ),
-        in_specs=[
-            pl.BlockSpec((2, block, state_size, page_width), lambda i: (0, i, 0, 0)),
-            pl.BlockSpec((2, block, state_size, half), lambda i: (0, i, 0, 0)),
+        in_specs=[pl.BlockSpec(memory_space=pl.ANY)] * 2,
+        out_specs=(pl.BlockSpec(memory_space=pl.ANY),) * 4,
+        scratch_shapes=[
+            pltpu.VMEM(early.shape, jnp.bfloat16),
+            pltpu.VMEM(late.shape, jnp.bfloat16),
+            pltpu.VMEM(wide, jnp.bfloat16),
+            pltpu.VMEM(wide, jnp.bfloat16),
+            pltpu.VMEM(paged, jnp.bfloat16),
+            pltpu.SemaphoreType.DMA((slots // 16, 4)),
+            pltpu.SemaphoreType.DMA((slots // 16, 5)),
         ],
-        out_specs=(
-            pl.BlockSpec((steps, block, width), lambda i: (0, i, 0)),
-            pl.BlockSpec((steps, block, width), lambda i: (0, i, 0)),
-            pl.BlockSpec((block, state_size, width), lambda i: (i, 0, 0)),
-            pl.BlockSpec((state_size + steps, block, page_width), lambda i: (0, i, 0)),
-        ),
         name="unpack",
         compiler_params=pltpu.CompilerParams(vmem_limit_bytes=60 << 20),
     )(early, late)
@@ -661,20 +680,14 @@
     d_skip,
 ):
     steps, width = mamba_in.shape[1], mamba_in.shape[3]
-    early, chosen = attention(
-        jnp.transpose(queries[:, :, 0], (1, 0, 2)),
-        jnp.transpose(new_kv[:, :, 0], (1, 0, 2)),
-        kv_cache[:, :, 0],
+    early, late = move_rows(
         lengths,
         destination[:, 0],
-        2 * lax.axis_size("replica"),
-        a_log.shape[0],
-    )
-    early, late = move_rows(
-        chosen,
-        early,
         jnp.transpose(mamba_in, (1, 2, 0, 3)),
         xproj_w.T,
+        kv_cache[:, :, 0],
+        jnp.transpose(new_kv[:, :, 0], (1, 0, 2)),
+        jnp.transpose(queries[:, :, 0], (1, 0, 2)),
         dtproj_w,
         dt_bias[None],
         a_log,

time: 101 us -> 95 us (0.941); the launches traced: 99.4 us -> 94.4 us
  Pallas kernels: 97.1 us -> 92.1 us
    pallas_call x2 -> x1, Pallas kernels: 8.16 us -> 3.34 us  [unpack(): pl.pallas_call(unpack_kernel, out_shape=(jax.ShapeDtypeStruct(wide, jnp.b...]
where the time goes in v6:
time: 95 us; the launch traced here: 94.4 us
  Pallas kernels  92.1 us (97%)
  local copies, waits for them, and re-layouts  1.64 us (2%)
    pallas_call x1, Pallas kernels, move_rows(): pl.pallas_call(move_kernel, out_shape=(jax.ShapeDtypeStruct(early_grid, j...  88.8 us
    pallas_call x1, Pallas kernels, unpack(): pl.pallas_call(unpack_kernel, out_shape=(jax.ShapeDtypeStruct(wide, jnp.b...  3.34 us

profile of v6, /device:TPU:6, one launch (start us, length us, event | category | flops | bytes accessed | tf_op | source)
XLA Modules:
  0.0 94.4 jit_solution(10706066110813806672)
XLA Ops:
  0.6 1.6 %copy.20 = bf16[16,3,2,1024]{3,0,2,1:T(8,128)(2,1)} copy(bf16[16,3,2,1024]{3,2,1,0:T(2,128)(2,1)} %param.12) | data formatting | bytes 393216 | tf_op args[0]
  2.3 88.8 %move_rows.1 = (bf16[2,8,8,16,256]{4,3,2,1,0:T(8,128)(2,1)}, bf16[2,8,8,16,640]{4,3,2,1,0:T(8,128)(2,1)}) custom-call(s32[16]{0:T(128)} %lengths.1, s32[16]{0:T(128)} %bitcast.36, bf16[3,2,16,1024]{3,2,1,0:T(8,128)(2,1)} %bitcast.30, bf16[544,1024]{1,0:T(8,128)(2,1)} %bitcast.28, bf16[16,16,256]{2,1,0:T(8,128)(2,1)} %bitcast.31, ...), custom_call_target="tpu_custom_call" | custom-call | tf_op jit(solution)/shard_map/move_rows/pallas_call | solution.py:526
  91.1 3.3 %unpack.1 = (bf16[3,64,1024]{2,1,0:T(8,128)(2,1)}, bf16[3,64,1024]{2,1,0:T(8,128)(2,1)}, bf16[64,16,1024]{2,1,0:T(8,128)(2,1)}, bf16[19,64,256]{2,1,0:T(8,128)(2,1)}) custom-call(bf16[2,64,16,256]{3,2,1,0:T(8,128)(2,1)} %bitcast.29, bf16[2,64,16,640]{3,2,1,0:T(8,128)(2,1)} %bitcast.27), custom_call_target="tpu_custom_call" | custom-call | tf_op jit(solution)/shard_map/unpack/pallas_call | solution.py:644

commit v7 on v6

--- a/solution.py
+++ b/solution.py
@@ -103,7 +103,7 @@
     state_in,
     out_early,
     out_late,
-    mamba,
+    mamba_rows,
     xproj,
     cached,
     fresh,
@@ -124,6 +124,7 @@
     readout,
     early,
     late,
+    mamba,
     bundles_early,
     bundles_late,
     table,
@@ -170,7 +171,7 @@
         pltpu.make_async_copy(source, held, loaded.at[index])
         for index, (source, held) in enumerate(
             [
-                (mamba_in, mamba),
+                (mamba_in, mamba_rows),
                 (xproj_in, xproj),
                 (cached_in, cached),
                 (fresh_in, fresh),
@@ -331,6 +332,9 @@
             pass_on(stage, route, 9, 4)
 
     loads[0].wait()
+    for step in range(steps):
+        for kind in range(2):
+            mamba[step, kind] = mamba_rows[:, step, kind].astype(jnp.float32).astype(jnp.bfloat16)
     loads[1].wait()
     chunk = part.shape[1]
     per_step = rows // chunk
@@ -509,7 +513,7 @@
 
 def move_rows(lengths, destination, *arrays):
     mamba, xproj_w, cached, a_log = arrays[0], arrays[1], arrays[2], arrays[7]
-    steps, _, rows, width = mamba.shape
+    rows, steps, _, width = mamba.shape
     state_size = a_log.shape[0]
     page_width = cached.shape[2]
     half = (width + page_width) // 2
@@ -546,6 +550,7 @@
             pltpu.VMEM((steps * rows, width), jnp.float32),
             pltpu.VMEM((2, rows + 1, state_size, page_width), jnp.bfloat16),
             pltpu.VMEM((2, rows + 1, state_size, half), jnp.bfloat16),
+            pltpu.VMEM((steps, 2, rows, width), jnp.bfloat16),
             pltpu.VMEM(kinds + (page_width,), jnp.bfloat16),
             pltpu.VMEM(kinds + (half,), jnp.bfloat16),
             pltpu.VMEM(table, jnp.int32),
@@ -683,7 +688,7 @@
     early, late = move_rows(
         lengths,
         destination[:, 0],
-        jnp.transpose(mamba_in, (1, 2, 0, 3)),
+        mamba_in,
         xproj_w.T,
         kv_cache[:, :, 0],
         jnp.transpose(new_kv[:, :, 0], (1, 0, 2)),

time: 95 us -> 93.3 us (0.982)
  local copies, waits for them, and re-layouts: 1.64 us -> 0 us
    unnamed x1 -> x0, local copies, waits for them, and re-layouts: 1.64 us -> none
where the time goes in v7:
time: 93.3 us; the launch traced here: 92.9 us
  Pallas kernels  92.2 us (99%)
    pallas_call x1, Pallas kernels, move_rows(): pl.pallas_call(move_kernel, out_shape=(jax.ShapeDtypeStruct(early_grid, j...  88.9 us
    pallas_call x1, Pallas kernels, unpack(): pl.pallas_call(unpack_kernel, out_shape=(jax.ShapeDtypeStruct(wide, jnp.b...  3.34 us

profile of v7, /device:TPU:6, one launch (start us, length us, event | category | flops | bytes accessed | tf_op | source)
XLA Modules:
  0.0 92.9 jit_solution(13195602897738940157)
XLA Ops:
  0.6 88.9 %move_rows.1 = (bf16[2,8,8,16,256]{4,3,2,1,0:T(8,128)(2,1)}, bf16[2,8,8,16,640]{4,3,2,1,0:T(8,128)(2,1)}) custom-call(s32[16]{0:T(128)} %lengths.1, s32[16]{0:T(128)} %bitcast.32, bf16[16,3,2,1024]{3,2,1,0:T(2,128)(2,1)} %mamba_in.1, bf16[544,1024]{1,0:T(8,128)(2,1)} %bitcast.25, bf16[16,16,256]{2,1,0:T(8,128)(2,1)} %bitcast.27, ...), custom_call_target="tpu_custom_call" | custom-call | tf_op jit(solution)/shard_map/move_rows/pallas_call | solution.py:530
  89.5 3.3 %unpack.1 = (bf16[3,64,1024]{2,1,0:T(8,128)(2,1)}, bf16[3,64,1024]{2,1,0:T(8,128)(2,1)}, bf16[64,16,1024]{2,1,0:T(8,128)(2,1)}, bf16[19,64,256]{2,1,0:T(8,128)(2,1)}) custom-call(bf16[2,64,16,256]{3,2,1,0:T(8,128)(2,1)} %bitcast.26, bf16[2,64,16,640]{3,2,1,0:T(8,128)(2,1)} %bitcast.24), custom_call_target="tpu_custom_call" | custom-call | tf_op jit(solution)/shard_map/unpack/pallas_call | solution.py:649
